TPU v7x, 128 devices: a whole 4x4x4 slice. The times are simulated.
128 devices in a mesh: group: 4 (over z), dev: 32 (over y, x, core).
Axes of the slice: x: 4, y: 4, z: 4, core: 2. Of those that a mesh axis runs over, the one named last changes fastest.
Arguments:
- store_states: bfloat16 [8192, 8, 2048], P(('group', 'dev')), may hold values from -6 to 6
- store_keys: bfloat16 [8192, 768], P(('group', 'dev')), may hold values from -6 to 6
- passage_ids: int32 [128, 32], replicated, may hold values from 0 to 8191, as said below
- store_slot: int32 [8192], replicated, may hold values from 0 to 8191, as said below
- row_question: int32 [4, 32], P('group'), may hold values from 0 to 31, each once within a row
- queries: bfloat16 [128, 8, 2048], P(('group', 'dev')), may hold values from -480 to 480
- question_emb: bfloat16 [128, 768], P(('group', 'dev')), may hold values from -6 to 6
- enc_gain: float32 [2048], replicated, may hold values from 0.5 to 1.5
- key_weight: bfloat16 [2048, 2048], replicated, may hold values from -0.125 to 0.125
- value_weight: bfloat16 [2048, 2048], replicated, may hold values from -0.125 to 0.125
Outputs:
- context: bfloat16 [128, 8, 2048], P(('group', 'dev'))
- distill_loss: float32 [128], P(('group', 'dev'))
- key_grad: float32 [8192, 768], P(('group', 'dev'))
Inputs may be any that keep to these rules, and one draw needn't show every extreme that they name: `passage_ids`: call the passages in slots k with k % (size of dev) = d of questions g * 32 to (g + 1) * 32 - 1 the requests of device (g, d); store row r lies on device r // 64 in group+dev order. All requests of one device lie on store devices of one group index; at most 2 of them lie on store devices of any one dev index; one store device holds at most 16 requests of the devices of one group. Both bounds are reached in every draw. `store_slot`: A permutation of the store rows. `row_question`: each row is a permutation of the questions of the group.
All inputs are finite; a program needn't handle non-finite values.
Results may differ from a plain program's by a relative error of at most 0.017.
The roundings to bfloat16 on the way count: a program that leaves them out, or rounds other values in their place, can miss the bound.
Values may be sent and summed in bfloat16 or wider, within the bound.
A program may use at most 128 MiB of HBM per device.

v0:
```python
import jax
import jax.numpy as jnp
from jax import lax
from jax.sharding import PartitionSpec as P

HEADS = 32


epsilon = 1e-06
loss_weight = 256.0


def rms_scale(states, enc_gain):
    values = states.astype(jnp.float32)
    mean_square = jnp.mean(values * values, axis=-1, keepdims=True)
    return (values * lax.rsqrt(mean_square + epsilon) * enc_gain).astype(jnp.bfloat16)


def earlier_same(labels):
    length_all = labels.shape[-1]
    matches = labels[..., :, None] == labels[..., None, :]
    before = jnp.arange(length_all)[:, None] < jnp.arange(length_all)[None, :]
    return jnp.sum((matches & before).astype(jnp.int32), axis=-2)


def place_rows(values, destination, extent):
    one_hot = (jnp.arange(extent)[:, None] == destination[None, :]).astype(values.dtype)
    return jnp.dot(one_hot, values, preferred_element_type=jnp.float32)


def body(
    store_states,
    store_keys,
    passage_ids,
    store_slot,
    row_question,
    queries,
    question_emb,
    enc_gain,
    key_weight,
    value_weight,
):
    group_count = lax.axis_size("group")
    dev_count = lax.axis_size("dev")
    devices = group_count * dev_count
    my_group = lax.axis_index("group")
    my_dev = lax.axis_index("dev")
    myself = my_group * dev_count + my_dev
    store_count = store_states.shape[0]
    passage_len = store_states.shape[1]
    model_width = store_states.shape[2]
    embed_dim = store_keys.shape[1]
    question_count, slot_count = passage_ids.shape
    per_group = question_count // group_count
    slot_share = slot_count // dev_count
    request_count = per_group * slot_share
    capacity = 2 * request_count // dev_count
    head_count = HEADS
    head_dim = model_width // head_count
    rows_here = queries.shape[0]
    answer = queries.shape[1]
    attn_scale = head_dim ** (-0.5)
    retrieval_scale = embed_dim ** (-0.5)
    store_rows = store_slot[passage_ids]
    layout = (
        store_rows.reshape(group_count, per_group, slot_share, dev_count)
        .transpose(0, 3, 1, 2)
        .reshape(devices, request_count)
    )
    owner_all = layout // store_count
    local_all = layout % store_count
    rank_all = earlier_same(owner_all)
    chosen = (owner_all[:, None, :] == myself) & (
        rank_all[:, None, :] == jnp.arange(capacity)[None, :, None]
    )
    send_local = jnp.sum(jnp.where(chosen, local_all[:, None, :], 0), axis=2)
    got_states, got_keys = (
        lax.all_to_all(
            store_states[send_local], ("group", "dev"), split_axis=0, concat_axis=0, tiled=True
        ),
        lax.all_to_all(
            store_keys[send_local], ("group", "dev"), split_axis=0, concat_axis=0, tiled=True
        ),
    )
    position = owner_all[myself] * capacity + rank_all[myself]
    states = got_states.reshape(devices * capacity, passage_len, model_width)[position]
    passage_keys = got_keys.reshape(devices * capacity, embed_dim)[position]
    normed = rms_scale(states, enc_gain).reshape(request_count * passage_len, model_width)
    key_cross = jnp.dot(normed, key_weight, preferred_element_type=jnp.float32).astype(jnp.bfloat16)
    value_cross = jnp.dot(normed, value_weight, preferred_element_type=jnp.float32).astype(
        jnp.bfloat16
    )
    key_cross = key_cross.reshape(per_group, slot_share, passage_len, model_width)
    value_cross = value_cross.reshape(per_group, slot_share, passage_len, model_width)
    passage_keys = passage_keys.reshape(per_group, slot_share, embed_dim)
    order_rows = row_question[0]
    key_in, value_in, retr_in = (
        lax.all_to_all(
            key_cross[order_rows].reshape(
                dev_count, rows_here, slot_share, passage_len, model_width
            ),
            "dev",
            split_axis=0,
            concat_axis=0,
            tiled=True,
        ),
        lax.all_to_all(
            value_cross[order_rows].reshape(
                dev_count, rows_here, slot_share, passage_len, model_width
            ),
            "dev",
            split_axis=0,
            concat_axis=0,
            tiled=True,
        ),
        lax.all_to_all(
            passage_keys[order_rows].reshape(dev_count, rows_here, slot_share, embed_dim),
            "dev",
            split_axis=0,
            concat_axis=0,
            tiled=True,
        ),
    )
    query_heads = queries.reshape(rows_here, answer, head_count, head_dim)
    key_heads = key_in.reshape(dev_count, rows_here, slot_share * passage_len, head_count, head_dim)
    value_heads = value_in.reshape(
        dev_count, rows_here, slot_share * passage_len, head_count, head_dim
    )
    scores = (
        jnp.einsum("rahe,drlhe->rhadl", query_heads, key_heads, preferred_element_type=jnp.float32)
        * attn_scale
    )
    peak_score = jnp.max(scores, axis=(3, 4), keepdims=True)
    exp_scores = jnp.exp(scores - peak_score)
    totals = jnp.sum(exp_scores, axis=(3, 4), keepdims=True)
    weights = exp_scores.astype(jnp.bfloat16)
    context = jnp.einsum(
        "rhadl,drlhe->rahe", weights, value_heads, preferred_element_type=jnp.float32
    )
    context = context / jnp.transpose(totals[..., 0, 0], (0, 2, 1))[..., None]
    passage_mass = jnp.sum(
        (exp_scores / totals).reshape(
            rows_here, head_count, answer, dev_count, slot_share, passage_len
        ),
        axis=(1, 2, 5),
    ) / (head_count * answer)
    passage_in = retr_in.transpose(1, 0, 2, 3)
    context_out = context.reshape(rows_here, answer, model_width).astype(jnp.bfloat16)
    retrieval = (
        jnp.einsum("rdke,re->rdk", passage_in, question_emb, preferred_element_type=jnp.float32)
        * retrieval_scale
    )
    log_prob = jax.nn.log_softmax(retrieval.reshape(rows_here, -1), axis=1).reshape(retrieval.shape)
    distill_loss = jnp.sum(passage_mass * (jnp.log(passage_mass) - log_prob), axis=(1, 2))
    coefficient = loss_weight * retrieval_scale * (jnp.exp(log_prob) - passage_mass)
    grad_rows = (
        coefficient[..., None] * question_emb.astype(jnp.float32)[:, None, None, :]
    ).astype(jnp.bfloat16)
    returned = lax.all_to_all(
        grad_rows.transpose(1, 0, 2, 3), "dev", split_axis=0, concat_axis=0, tiled=True
    )
    reorder = (order_rows[None, :] == jnp.arange(per_group)[:, None]).astype(jnp.bfloat16)
    grad_req = jnp.dot(
        reorder,
        returned.reshape(per_group, slot_share * embed_dim),
        preferred_element_type=jnp.float32,
    )
    grad_req = grad_req.astype(jnp.bfloat16)
    slots_back = place_rows(
        grad_req, owner_all[myself] * capacity + rank_all[myself], devices * capacity
    )
    slots_back = slots_back.astype(jnp.bfloat16).reshape(devices, capacity, embed_dim)
    arrived = lax.all_to_all(slots_back, ("group", "dev"), split_axis=0, concat_axis=0, tiled=True)
    key_grad = place_rows(
        arrived.reshape(devices * capacity, embed_dim), send_local.reshape(-1), store_count
    )
    return (context_out, distill_loss, key_grad)


def solution(mesh):
    in_specs = (
        P(("group", "dev"), None, None),
        P(("group", "dev"), None),
        P(),
        P(),
        P("group", None),
        P(("group", "dev"), None, None),
        P(("group", "dev"), None),
        P(),
        P(),
        P(),
    )
    out_specs = (P(("group", "dev"), None, None), P(("group", "dev")), P(("group", "dev"), None))
    return jax.shard_map(body, mesh=mesh, in_specs=in_specs, out_specs=out_specs, check_vma=False)
```

profile of v0, /device:TPU:0, one launch (start us, length us, event | category | flops | bytes accessed | tf_op | source)
XLA Modules:
  0.0 275.4 jit_solution(11804137417681160382)
XLA Ops:
  1.7 23.0 %gather_fusion = s32[4096]{0:T(1024)S(1)} fusion(s32[8192]{0:T(1024)S(1)} %copy-done.1, s32[4096]{0:T(1024)S(1)} %broadcast_clamp_fusion), kind=kCustom, calls=%fused_computation | custom fusion | bytes 49152 | tf_op jit(solution)/shard_map/gather | solution.py:64
  26.2 1.2 gather_fusion.5
  27.4 0.9 reshape.475
  28.3 11.1 %all-to-all-start.3 = ((bf16[128,2,768]{2,1,0:T(2,128)(2,1)}), bf16[128,2,768]{2,1,0:T(2,128)(2,1)S(1)}, u32[]{:S(2)}, u32[]{:S(2)}) async-start(bf16[128,2,768]{2,1,0:T(2,128)(2,1)} %reshape.475), calls=%async_computation.3 | async-start | bytes 786432 | tf_op jit(solution)/shard_map/all_to_all | solution.py:81
  39.5 8.3 %gather_fusion.1 = bf16[256,8,2048]{2,1,0:T(8,128)(2,1)} fusion(bf16[64,8,2048]{2,1,0:T(8,128)(2,1)S(1)} %copy-done, s32[1024]{0:T(1024)S(1)} %pad_clamp_fusion.2), kind=kCustom, calls=%fused_computation.1 | custom fusion | bytes 16778240 | tf_op jit(solution)/shard_map/gather | solution.py:79
  47.8 3.8 %all-to-all-done.3 = bf16[128,2,768]{2,1,0:T(2,128)(2,1)S(1)} async-done(((bf16[128,2,768]{2,1,0:T(2,128)(2,1)}), bf16[128,2,768]{2,1,0:T(2,128)(2,1)S(1)}, u32[]{:S(2)}, u32[]{:S(2)}) %all-to-all-start.3) | async-done | bytes 393248 | tf_op jit(solution)/shard_map/all_to_all | solution.py:81
  51.6 6.5 %all-to-all-start = ((bf16[128,2,8,2048]{3,2,1,0:T(8,128)(2,1)}), bf16[128,2,8,2048]{3,2,1,0:T(8,128)(2,1)}, u32[]{:S(2)}, u32[]{:S(2)}) async-start(bf16[128,2,8,2048]{3,2,1,0:T(8,128)(2,1)} %bitcast.81), calls=%async_computation | async-start | bytes 16777216 | tf_op jit(solution)/shard_map/all_to_all | solution.py:78
  62.1 94.4 %all-to-all-done = bf16[128,2,8,2048]{3,2,1,0:T(8,128)(2,1)} async-done(((bf16[128,2,8,2048]{3,2,1,0:T(8,128)(2,1)}), bf16[128,2,8,2048]{3,2,1,0:T(8,128)(2,1)}, u32[]{:S(2)}, u32[]{:S(2)}) %all-to-all-start) | async-done | bytes 8388640 | tf_op jit(solution)/shard_map/all_to_all | solution.py:78
  156.5 9.3 %all-to-all-start.4 = ((bf16[32,2,384]{2,1,0:T(2,128)(2,1)}), bf16[32,2,384]{2,1,0:T(2,128)(2,1)S(1)}, u32[]{:S(2)}, u32[]{:S(2)}) async-start(bf16[32,2,384]{2,1,0:T(2,128)(2,1)} %reshape.519), calls=%async_computation.4 | async-start | bytes 98304 | tf_op jit(solution)/shard_map/all_to_all | solution.py:116
  165.8 4.0 %gather_fusion.2 = bf16[32,8,2048]{2,1,0:T(8,128)(2,1)S(1)} fusion(bf16[256,8,2048]{2,1,0:T(8,128)(2,1)} %bitcast.3, s32[1024]{0:T(1024)S(1)} %pad_clamp_fusion.1), kind=kCustom, calls=%fused_computation.2 | custom fusion | bytes 2097280 | tf_op jit(solution)/shard_map/gather | solution.py:86
  170.2 6.8 %fusion.1 = bf16[32,8,2048]{2,1,0:T(8,128)(2,1)} fusion(bf16[2048,2048]{1,0:T(8,128)(2,1)} %param.18, bf16[32,8,2048]{2,1,0:T(8,128)(2,1)S(1)} %gather_fusion.2, f32[2048]{0:T(1024)S(1)} %copy-done.13, f32[256]{0:T(256)S(1)} %rsqrt.12), kind=kOutput, calls=%fused_computation.13 | convolution fusion | flops 2150105088 | bytes 10494976 | tf_op jit(solution)/shard_map/dot_general | solution.py:89
  177.0 2.9 %gather_fusion.4 = bf16[32,8,2048]{2,1,0:T(8,128)(2,1)} fusion(bf16[32,8,2048]{2,1,0:T(8,128)(2,1)} %fusion.1, s32[1024]{0:T(1024)S(1)} %pad_clamp_fusion), kind=kCustom, calls=%fused_computation.4 | custom fusion | bytes 2097280 | tf_op jit(solution)/shard_map/gather | solution.py:99
  179.8 7.6 %all-to-all-start.2 = ((bf16[32,1,1,8,2048]{4,3,2,1,0:T(8,128)(2,1)}), bf16[32,1,1,8,2048]{4,3,2,1,0:T(8,128)(2,1)S(1)}, u32[]{:S(2)}, u32[]{:S(2)}) async-start(bf16[32,1,1,8,2048]{4,3,2,1,0:T(8,128)(2,1)} %bitcast.82), calls=%async_computation.2 | async-start | bytes 2097152 | tf_op jit(solution)/shard_map/all_to_all | solution.py:98
  188.4 1.2 exponential_reduce_fusion
  190.3 14.2 %all-to-all-done.2 = bf16[32,1,1,8,2048]{4,3,2,1,0:T(8,128)(2,1)S(1)} async-done(((bf16[32,1,1,8,2048]{4,3,2,1,0:T(8,128)(2,1)}), bf16[32,1,1,8,2048]{4,3,2,1,0:T(8,128)(2,1)S(1)}, u32[]{:S(2)}, u32[]{:S(2)}) %all-to-all-start.2) | async-done | bytes 1048608 | tf_op jit(solution)/shard_map/all_to_all | solution.py:98
  204.6 3.2 %reshape.419 = bf16[32,8,32,64]{3,2,1,0:T(8,128)(2,1)} reshape(bf16[32,1,1,8,2048]{4,3,2,1,0:T(8,128)(2,1)S(1)} %all-to-all-done.2) | data formatting | bytes 2097152 | tf_op jit(solution)/shard_map/reshape.1
  207.8 4.5 %fusion.50 = (f32[32,8]{1,0:T(8,128)S(1)}, f32[32,8,32,8]{2,1,3,0:T(8,128)S(1)}) fusion(bf16[8,32,64,1]{2,1,0,3:T(8,128)(2,1)S(1)} %bitcast.87, bf16[32,8,32,64]{3,2,1,0:T(8,128)(2,1)} %reshape.419), kind=kOutput, calls=%fused_computation.80 | convolution fusion | flops 8519424 | bytes 1344512 | tf_op jit(solution)/shard_map/rahe,drlhe->rhadl/dot_general | solution.py:130
  213.8 1.3 subtract_multiply_fusion
  216.4 3.9 %all-to-all-start.5 = ((bf16[32,2,384]{2,1,0:T(2,128)(2,1)}), bf16[32,2,384]{2,1,0:T(2,128)(2,1)S(1)}, u32[]{:S(2)}, u32[]{:S(2)}) async-start(bf16[32,2,384]{2,1,0:T(2,128)(2,1)} %reshape.521), calls=%async_computation.5 | async-start | bytes 98304 | tf_op jit(solution)/shard_map/all_to_all | solution.py:159
  220.3 6.8 %fusion = bf16[32,8,2048]{2,1,0:T(8,128)(2,1)} fusion(bf16[2048,2048]{1,0:T(8,128)(2,1)} %param.19, bf16[32,8,2048]{2,1,0:T(8,128)(2,1)S(1)} %copy-done.4, f32[2048]{0:T(1024)S(1)} %copy-done.13, f32[256]{0:T(256)S(1)} %rsqrt.12), kind=kOutput, calls=%fused_computation.12 | convolution fusion | flops 2150105088 | bytes 10494976 | tf_op jit(solution)/shard_map/dot_general | solution.py:90
  227.1 2.8 %gather_fusion.3 = bf16[32,8,2048]{2,1,0:T(8,128)(2,1)} fusion(bf16[32,8,2048]{2,1,0:T(8,128)(2,1)} %fusion, s32[1024]{0:T(1024)S(1)} %pad_clamp_fusion), kind=kCustom, calls=%fused_computation.3 | custom fusion | bytes 2097280 | tf_op jit(solution)/shard_map/gather | solution.py:108
  229.9 7.4 %all-to-all-start.1 = ((bf16[32,1,1,8,2048]{4,3,2,1,0:T(8,128)(2,1)}), bf16[32,1,1,8,2048]{4,3,2,1,0:T(8,128)(2,1)S(1)}, u32[]{:S(2)}, u32[]{:S(2)}) async-start(bf16[32,1,1,8,2048]{4,3,2,1,0:T(8,128)(2,1)} %bitcast.83), calls=%async_computation.1 | async-start | bytes 2097152 | tf_op jit(solution)/shard_map/all_to_all | solution.py:107
  238.0 1.3 convolution_convert_fusion.2
  239.3 0.9 reshape.427
  240.2 14.5 %all-to-all-done.1 = bf16[32,1,1,8,2048]{4,3,2,1,0:T(8,128)(2,1)S(1)} async-done(((bf16[32,1,1,8,2048]{4,3,2,1,0:T(8,128)(2,1)}), bf16[32,1,1,8,2048]{4,3,2,1,0:T(8,128)(2,1)S(1)}, u32[]{:S(2)}, u32[]{:S(2)}) %all-to-all-start.1) | async-done | bytes 1048608 | tf_op jit(solution)/shard_map/all_to_all | solution.py:107
  254.7 7.6 %all-to-all-start.6 = ((bf16[128,2,768]{2,1,0:T(2,128)(2,1)}), bf16[128,2,768]{2,1,0:T(2,128)(2,1)S(1)}, u32[]{:S(2)}, u32[]{:S(2)}) async-start(bf16[128,2,768]{2,1,0:T(2,128)(2,1)} %reshape.427), calls=%async_computation.6 | async-start | bytes 786432 | tf_op jit(solution)/shard_map/all_to_all | solution.py:173
  262.2 1.4 copy.81
  263.6 1.5 eq.91
  265.1 3.2 %reshape.416 = bf16[32,8,32,64]{3,2,1,0:T(8,128)(2,1)} reshape(bf16[32,1,1,8,2048]{4,3,2,1,0:T(8,128)(2,1)S(1)} %all-to-all-done.1) | data formatting | bytes 2097152 | tf_op jit(solution)/shard_map/reshape.4
  268.3 3.6 %fusion.22 = bf16[1,8,32,64]{3,1,2,0:T(8,128)(2,1)S(1)} fusion(bf16[32,8,32,64]{3,2,1,0:T(8,128)(2,1)} %reshape.416, f32[32,8,32,8]{2,1,3,0:T(8,128)} %copy-done.5, f32[32,8]{1,0:T(8,128)S(1)} %get-tuple-element.7, f32[8,32]{0,1:T(8,128)} %bitcast.86), kind=kOutput, calls=%fused_computation.27 | convolution fusion | flops 8552448 | bytes 1345536 | tf_op jit(solution)/shard_map/rhadl,drlhe->rahe/dot_general | solution.py:137
  272.7 1.7 all-to-all-done.6
  274.5 0.9 fusion.34
  (73 shorter events, 12.2 us)
Async XLA Ops:
  0.6 38.8 %copy-start = (bf16[64,8,2048]{2,1,0:T(8,128)(2,1)S(1)}, bf16[64,8,2048]{2,1,0:T(8,128)(2,1)}, u32[]{:S(2)}) copy-start(bf16[64,8,2048]{2,1,0:T(8,128)(2,1)} %param.10) | copy-start | bytes 6291460
  0.6 1.1 copy-start.1
  24.8 1.4 copy-start.2
  25.3 0.6 copy-start.8
  28.3 23.3 %all-to-all-start.3 = ((bf16[128,2,768]{2,1,0:T(2,128)(2,1)}), bf16[128,2,768]{2,1,0:T(2,128)(2,1)S(1)}, u32[]{:S(2)}, u32[]{:S(2)}) async-start(bf16[128,2,768]{2,1,0:T(2,128)(2,1)} %reshape.475), calls=%async_computation.3 | async-start | bytes 786432 | tf_op jit(solution)/shard_map/all_to_all | solution.py:81
  51.6 6.7 %copy-start.12 = (s32[1,32]{1,0:T(1,128)S(1)}, s32[1,32]{1,0:T(1,128)}, u32[]{:S(2)}) copy-start(s32[1,32]{1,0:T(1,128)} %param.14) | copy-start | bytes 388
  51.6 104.9 %all-to-all-start = ((bf16[128,2,8,2048]{3,2,1,0:T(8,128)(2,1)}), bf16[128,2,8,2048]{3,2,1,0:T(8,128)(2,1)}, u32[]{:S(2)}, u32[]{:S(2)}) async-start(bf16[128,2,8,2048]{3,2,1,0:T(8,128)(2,1)} %bitcast.81), calls=%async_computation | async-start | bytes 16777216 | tf_op jit(solution)/shard_map/all_to_all | solution.py:78
  58.3 0.6 copy-start.9
  59.0 111.2 %copy-start.13 = (f32[2048]{0:T(1024)S(1)}, f32[2048]{0:T(1024)}, u32[]{:S(2)}) copy-start(f32[2048]{0:T(1024)} %param.17) | copy-start | bytes 24580
  156.5 23.4 %all-to-all-start.4 = ((bf16[32,2,384]{2,1,0:T(2,128)(2,1)}), bf16[32,2,384]{2,1,0:T(2,128)(2,1)S(1)}, u32[]{:S(2)}, u32[]{:S(2)}) async-start(bf16[32,2,384]{2,1,0:T(2,128)(2,1)} %reshape.519), calls=%async_computation.4 | async-start | bytes 98304 | tf_op jit(solution)/shard_map/all_to_all | solution.py:116
  169.8 7.2 %copy-start.3 = (bf16[32,8,2048]{2,1,0:T(8,128)(2,1)}, bf16[32,8,2048]{2,1,0:T(8,128)(2,1)S(1)}, u32[]{:S(2)}) copy-start(bf16[32,8,2048]{2,1,0:T(8,128)(2,1)S(1)} %gather_fusion.2) | copy-start | bytes 3145732
  177.0 10.5 %copy-start.7 = (bf16[1,8,2048]{2,1,0:T(8,128)(2,1)S(1)}, bf16[1,8,2048]{2,1,0:T(8,128)(2,1)}, u32[]{:S(2)}) copy-start(bf16[1,8,2048]{2,1,0:T(8,128)(2,1)} %param.15) | copy-start | bytes 98308
  177.0 10.6 %copy-start.11 = (bf16[1,768]{1,0:T(2,128)(2,1)S(1)}, bf16[1,768]{1,0:T(2,128)(2,1)}, u32[]{:S(2)}) copy-start(bf16[1,768]{1,0:T(2,128)(2,1)} %param.16) | copy-start | bytes 4612
  179.8 24.7 %all-to-all-start.2 = ((bf16[32,1,1,8,2048]{4,3,2,1,0:T(8,128)(2,1)}), bf16[32,1,1,8,2048]{4,3,2,1,0:T(8,128)(2,1)S(1)}, u32[]{:S(2)}, u32[]{:S(2)}) async-start(bf16[32,1,1,8,2048]{4,3,2,1,0:T(8,128)(2,1)} %bitcast.82), calls=%async_computation.2 | async-start | bytes 2097152 | tf_op jit(solution)/shard_map/all_to_all | solution.py:98
  212.3 1.0 copy-start.5
  212.3 8.0 %copy-start.4 = (bf16[32,8,2048]{2,1,0:T(8,128)(2,1)S(1)}, bf16[32,8,2048]{2,1,0:T(8,128)(2,1)}, u32[]{:S(2)}) copy-start(bf16[32,8,2048]{2,1,0:T(8,128)(2,1)} %copy-done.3) | copy-start | bytes 3145732
  213.3 1.8 copy-start.6
  216.4 13.5 %all-to-all-start.5 = ((bf16[32,2,384]{2,1,0:T(2,128)(2,1)}), bf16[32,2,384]{2,1,0:T(2,128)(2,1)S(1)}, u32[]{:S(2)}, u32[]{:S(2)}) async-start(bf16[32,2,384]{2,1,0:T(2,128)(2,1)} %reshape.521), calls=%async_computation.5 | async-start | bytes 98304 | tf_op jit(solution)/shard_map/all_to_all | solution.py:159
  229.9 24.7 %all-to-all-start.1 = ((bf16[32,1,1,8,2048]{4,3,2,1,0:T(8,128)(2,1)}), bf16[32,1,1,8,2048]{4,3,2,1,0:T(8,128)(2,1)S(1)}, u32[]{:S(2)}, u32[]{:S(2)}) async-start(bf16[32,1,1,8,2048]{4,3,2,1,0:T(8,128)(2,1)} %bitcast.83), calls=%async_computation.1 | async-start | bytes 2097152 | tf_op jit(solution)/shard_map/all_to_all | solution.py:107
  254.7 19.7 %all-to-all-start.6 = ((bf16[128,2,768]{2,1,0:T(2,128)(2,1)}), bf16[128,2,768]{2,1,0:T(2,128)(2,1)S(1)}, u32[]{:S(2)}, u32[]{:S(2)}) async-start(bf16[128,2,768]{2,1,0:T(2,128)(2,1)} %reshape.427), calls=%async_computation.6 | async-start | bytes 786432 | tf_op jit(solution)/shard_map/all_to_all | solution.py:173
  268.3 6.2 %copy-start.10 = (s32[256]{0:T(256)S(1)}, s32[256]{0:T(256)}, u32[]{:S(2)}) copy-start(s32[256]{0:T(256)} %eq.91) | copy-start | bytes 3076
where the time goes:
time: 277 us; the launch traced here: 275 us
  waiting for transfers between devices  129 us (47%)
  local copies, waits for them, and re-layouts  60.9 us (22%)
  starting transfers between devices  53.3 us (19%)
  matrix products  24.6 us (9%)
  other arithmetic  6.4 us (2%)
    all_to_all x1, waiting for transfers between devices, body(): lax.all_to_all(store_states[send_local], ('group', 'dev'), split_axis=0,...  94.4 us
    gather x1, local copies, waits for them, and re-layouts, body(): store_rows = store_slot[passage_ids]  23 us
    all_to_all x1, waiting for transfers between devices, body(): lax.all_to_all(value_cross[order_rows].reshape(dev_count, rows_here, slot...  14.5 us
    all_to_all x1, waiting for transfers between devices, body(): lax.all_to_all(key_cross[order_rows].reshape(dev_count, rows_here, slot_s...  14.2 us
    all_to_all x1, starting transfers between devices, body(): lax.all_to_all(store_keys[send_local], ('group', 'dev'), split_axis=0, co...  11.1 us
    all_to_all x1, starting transfers between devices, body(): lax.all_to_all(passage_keys[order_rows].reshape(dev_count, rows_here, slo...  9.3 us
    gather x1, local copies, waits for them, and re-layouts, body(): store_states[send_local]  8.31 us
    all_to_all x1, starting transfers between devices, body(): lax.all_to_all(key_cross[order_rows].reshape(dev_count, rows_here, slot_s...  7.56 us
  transfers between devices with their start and end apart: 7, of which 5 were waited for; matrix products, arithmetic and copies ran while one was open for 18% of the time, Pallas kernels for 0%

commit v1 on v0

v1 whole, which is shorter than its diff:
```python
import functools

import jax
import jax.numpy as jnp
from jax import lax
from jax.experimental import pallas as pl
from jax.experimental.pallas import tpu as pltpu
from jax.sharding import PartitionSpec as P

MESH = pl.DeviceIdType.MESH
F32 = jnp.float32
BF16 = jnp.bfloat16
HIGHEST = lax.Precision.HIGHEST

D = 2048
E = 768
GROUPS = 4
PER_GROUP = 32
SLOTS = 16
LANES = 128
STORE = 64
EPS = 1e-06
LOSS_WEIGHT = 256.0
ABSENT = -1e30

ORDERS = (("x", "y", "z"), ("y", "z", "x"), ("z", "x", "y"))
AG, AG_SIB, RQ, AR, RS = 0, 27, 39, 42, 75
SEMS = 105


def nt(a, b, precision=None):
    return lax.dot_general(
        a, b, (((1,), (1,)), ((), ())), preferred_element_type=F32, precision=precision
    )


def nn(a, b, precision=None):
    return jnp.dot(a, b, preferred_element_type=F32, precision=precision)


def iota(shape, dim):
    return lax.broadcasted_iota(jnp.int32, shape, dim)


def block_of(part, g, j):
    y, x, core = j // 8, (j // 2) % 4, j % 2
    at = {"x": x, "y": y, "z": g}
    first, second, third = ORDERS[part]
    return core * 64 + at[third] * 16 + at[second] * 4 + at[first]


def add_blocks(part, blocks):
    total = blocks[0].astype(F32)
    for block in blocks[1:]:
        total = total + block.astype(F32)
    if part < 2:
        return total, total.astype(BF16)
    loss = total[0:8, 256:384] + total[8:16, 256:384]
    high = loss.astype(BF16).astype(F32)
    tile = jnp.concatenate([high, loss - high], axis=0)
    return total, jnp.concatenate([total[:, 0:256], tile], axis=1).astype(BF16)


def kernel(
    rows_ref,
    lane_ref,
    col_ref,
    own_rq_ref,
    states_ref,
    keys_ref,
    queries_ref,
    emb_ref,
    gain_ref,
    kw_ref,
    vw_ref,
    ctx_ref,
    loss_ref,
    grad_ref,
    st,
    w,
    nrm,
    kv,
    q0,
    q1,
    q2,
    c0,
    c1,
    c2,
    rc0,
    rc1,
    rc2,
    ra0,
    ra1,
    ra2,
    rb0,
    rb1,
    rb2,
    rd0,
    rd1,
    rd2,
    s_buf,
    p_buf,
    t0,
    t1,
    t2,
    ac0,
    ac1,
    ac2,
    ar0,
    ar1,
    ar2,
    acc0,
    acc1,
    acc2,
    l0,
    l1,
    l2,
    rqt,
    ir_ref,
    loss_t,
    send_sem,
    recv_sem,
    local_sem,
):
    qs, cs, rcs = (q0, q1, q2), (c0, c1, c2), (rc0, rc1, rc2)
    rstage = ((ra0, ra1, ra2), (rb0, rb1, rb2), (rd0, rd1, rd2))
    ts, acs, ars, accs, ls = (
        (t0, t1, t2),
        (ac0, ac1, ac2),
        (ar0, ar1, ar2),
        (acc0, acc1, acc2),
        (l0, l1, l2),
    )
    my_group = lax.axis_index("group")
    my_dev = lax.axis_index("dev")
    core = my_dev % 2
    at = {"x": (my_dev // 2) % 4, "y": my_dev // 8, "z": my_group}
    sibling = (my_group, my_dev + 1 - 2 * core)

    def peer(axis, step):
        to = (at[axis] + step) % 4
        if axis == "z":
            return (to, my_dev)
        if axis == "y":
            return (my_group, to * 8 + at["x"] * 2 + core)
        return (my_group, at["y"] * 8 + to * 2 + core)

    started = []

    def remote(src, dst, number, device):
        copy = pltpu.make_async_remote_copy(
            src_ref=src,
            dst_ref=dst,
            send_sem=send_sem.at[number],
            recv_sem=recv_sem.at[number],
            device_id=device,
            device_id_type=MESH,
        )
        return copy

    def start(src, dst, number, device):
        copy = remote(src, dst, number, device)
        copy.start()
        started.append(copy)

    def arrived(dst, number):
        remote(dst, dst, number, sibling).wait_recv()

    states_copy = pltpu.make_async_copy(states_ref, st, local_sem.at[8])
    states_copy.start()
    w_copies = []
    for n in range(8):
        src = kw_ref if n < 4 else vw_ref
        copy = pltpu.make_async_copy(
            src.at[:, pl.ds((n % 4) * 512, 512)],
            w.at[:, pl.ds(n * 512, 512)],
            local_sem.at[n],
        )
        copy.start()
        w_copies.append(copy)

    mine = [
        core * 64 + at[ORDERS[p][2]] * 16 + at[ORDERS[p][1]] * 4 + at[ORDERS[p][0]]
        for p in range(3)
    ]
    for c in range(8):
        tile = jnp.concatenate(
            [
                queries_ref[0, :, c * 128 : c * 128 + 128].astype(F32),
                queries_ref[0, :, 1024 + c * 128 : 1152 + c * 128].astype(F32),
            ],
            axis=0,
        )
        qs[c // 3][mine[c // 3], :, (c % 3) * 128 : (c % 3) * 128 + 128] = tile.astype(BF16)
    emb_rows = [emb_ref[:, c * 128 : c * 128 + 128].astype(F32) for c in range(6)]
    emb_tile = jnp.concatenate(emb_rows + [jnp.zeros((10, 128), F32)], axis=0)
    q2[mine[2], :, 256:384] = emb_tile.astype(BF16)
    rqt[my_group] = own_rq_ref[...]

    barrier = pltpu.get_barrier_semaphore()
    pl.semaphore_signal(barrier, inc=1, device_id=sibling, device_id_type=MESH)
    for axis in ("x", "y", "z"):
        for step in (1, 2, 3):
            pl.semaphore_signal(barrier, inc=1, device_id=peer(axis, step), device_id_type=MESH)
    pl.semaphore_wait(barrier, 10)

    def span(p, stage, back):
        first, second, third = ORDERS[p]
        digit = (at[ORDERS[p][stage]] + 4 - back) % 4
        if stage == 0:
            return core * 64 + at[third] * 16 + at[second] * 4 + digit, 1
        if stage == 1:
            return core * 64 + at[third] * 16 + digit * 4, 4
        return core * 64 + digit * 16, 16

    def gather_start(stage):
        for p in range(3):
            begin, size = span(p, stage, 0)
            for step in (1, 2, 3):
                ref = qs[p].at[pl.ds(begin, size)]
                start(ref, ref, AG + (p * 3 + stage) * 3 + step - 1, peer(ORDERS[p][stage], step))

    def gather_wait(p, stage, step):
        begin, size = span(p, stage, step)
        arrived(qs[p].at[pl.ds(begin, size)], AG + (p * 3 + stage) * 3 + step - 1)

    def forward(p, back):
        begin, size = span(p, 2, back)
        ref = qs[p].at[pl.ds(begin, size)]
        start(ref, ref, AG_SIB + p * 4 + back, sibling)

    gather_start(0)
    for step in (1, 2, 3):
        start(own_rq_ref, rqt.at[my_group], RQ + step - 1, peer("z", step))

    states_copy.wait()

    def norm_pair(pair, carry):
        both = []
        for half in range(2):
            values = st[rows_ref[pair * 2 + half]].astype(F32)
            mean_square = jnp.mean(values * values, axis=-1, keepdims=True)
            both.append(values * lax.rsqrt(mean_square + EPS) * gain_ref[...])
        nrm[pl.ds(pl.multiple_of(pair * 16, 16), 16), :] = jnp.concatenate(both, axis=0).astype(BF16)
        return carry

    lax.fori_loop(0, 32, norm_pair, 0)

    def project(begin, end):
        def step(n, carry):
            offset = pl.multiple_of(n * 256, 256)
            kv[:, pl.ds(offset, 256)] = nn(nrm[...], w[:, pl.ds(offset, 256)]).astype(BF16)
            return carry

        for n in range(begin, end):
            w_copies[n].wait()
        lax.fori_loop(begin * 2, end * 2, step, 0)

    for p in range(3):
        for step in (1, 2, 3):
            gather_wait(p, 0, step)
    gather_start(1)
    project(0, 2)
    for p in range(3):
        for step in (1, 2, 3):
            gather_wait(p, 1, step)
    gather_start(2)
    for p in range(3):
        forward(p, 0)
    project(2, 6)
    for step in (1, 3, 2):
        for p in range(3):
            gather_wait(p, 2, step)
            forward(p, step)
    project(6, 8)

    for step in (1, 2, 3):
        arrived(rqt.at[(my_group + 4 - step) % 4], RQ + step - 1)
    for g in range(4):
        match = rqt[g, 0:32, :] == lane_ref[g : g + 1, :]
        row = jnp.sum(jnp.where(match, iota((32, 128), 0) + (g * 32 + 1), 0), axis=0, keepdims=True)
        ir_ref[g : g + 1, :] = row - 1

    for p in range(3):
        for back in range(4):
            first, second, third = ORDERS[p]
            begin = (1 - core) * 64 + ((at[third] + 4 - back) % 4) * 16
            arrived(qs[p].at[pl.ds(begin, 16)], AG_SIB + p * 4 + back)

    lane = iota((1, 128), 1)
    low = (lane < 64).astype(F32).astype(BF16)
    high = (lane >= 64).astype(F32).astype(BF16)

    def scores_of(p, tiles):
        def step(n, carry):
            g, cc = n // tiles, n % tiles
            inner = pl.multiple_of(cc * 128, 128)
            outer = pl.multiple_of((3 * p + cc) * 128, 128)
            slots = pl.ds(pl.multiple_of(g * 128, 128), 128)
            right = jnp.concatenate(
                [kv[slots, pl.ds(outer, 128)], kv[slots, pl.ds(outer + 1024, 128)]], axis=0
            )
            row = ir_ref[pl.ds(g, 1), :] - g * 32
            total = [jnp.zeros((8, 128), F32) for _ in range(4)]
            for jb in range(2):
                left = []
                for jj in range(16):
                    block = qs[p][block_of(p, g, jb * 16 + jj), :, pl.ds(inner, 128)]
                    left += [block * low, block * high]
                out = nt(jnp.concatenate(left, axis=0), right)
                for jj in range(16):
                    keep = jnp.broadcast_to(row == jb * 16 + jj, (8, 128))
                    for tile in range(4):
                        half = tile % 2
                        begin = jj * 32 + tile * 8
                        piece = out[begin : begin + 8, half * 128 : half * 128 + 128]
                        total[tile] = jnp.where(keep, piece, total[tile])
            rows = pl.ds(pl.multiple_of((3 * p + cc) * 32, 32), 32)
            s_buf[g, rows, :] = jnp.concatenate(total, axis=0) * (64 ** (-0.5))
            return carry

        lax.fori_loop(0, 4 * tiles, step, 0)

    scores_of(0, 3)
    scores_of(1, 3)
    scores_of(2, 2)

    sub = iota((128, 128), 0)
    lanes = iota((128, 128), 1)
    peak_i = jnp.zeros((256, 128), F32)
    total_i = jnp.zeros((256, 128), F32)
    present = jnp.zeros((8, 128), F32)
    for g in range(4):
        scores = s_buf[g]
        u_row = lane_ref[g : g + 1, :]
        peak = scores
        for s in (1, 2, 4):
            bit = jnp.broadcast_to((lane // s) % 2 == 1, (256, 128))
            other = jnp.where(bit, pltpu.roll(peak, s, 1), pltpu.roll(peak, 128 - s, 1))
            peak = jnp.maximum(peak, other)
        u_rows = jnp.broadcast_to(u_row, (8, 128))
        before = pltpu.roll(u_rows, 8, 1)[0:1, :]
        for s in (8, 16, 32, 64):
            same = (pltpu.roll(u_rows, s, 1)[0:1, :] == u_row) & (lane >= s)
            other = jnp.where(jnp.broadcast_to(same, (256, 128)), pltpu.roll(peak, s, 1), ABSENT)
            peak = jnp.maximum(peak, other)
        for s in (8, 16, 32, 64):
            same = (pltpu.roll(u_rows, 128 - s, 1)[0:1, :] == u_row) & (lane < 128 - s)
            other = jnp.where(
                jnp.broadcast_to(same, (256, 128)), pltpu.roll(peak, 128 - s, 1), ABSENT
            )
            peak = jnp.maximum(peak, other)
        chosen = sub == ir_ref[g : g + 1, :]
        first = ((before != u_row) | (lane < 8)) & (lane % 8 == 0)
        lead = jnp.where(chosen & jnp.broadcast_to(first, (128, 128)), 1.0, 0.0)
        peak_i = peak_i + nt(peak, lead, HIGHEST)
        total_i = total_i + nt(jnp.exp(scores - peak), jnp.where(chosen, 1.0, 0.0), HIGHEST)
        present = present + nt(jnp.ones((8, 128), F32), lead)
    table = jnp.where(
        jnp.broadcast_to(present[0:1, :] > 0.5, (256, 128)),
        peak_i + jnp.log(jnp.maximum(total_i, 1e-30)),
        ABSENT,
    )
    t0[...] = table[0:128, :]
    t1[...] = table[128:256, :]

    u_col = jnp.concatenate([col_ref[:, 0:1]], axis=0)
    k_col = col_ref[:, 1:2]
    row_col = col_ref[:, 2:3]
    valid = u_col >= 0
    lane64 = iota((64, 128), 1)
    slot_group = iota((64, 128), 0) // 16
    row_question = jnp.concatenate(
        [jnp.broadcast_to(rqt[g, 32:33, :], (16, 128)) for g in range(4)], axis=0
    )
    one_hot_i = (row_question == u_col) & (lane64 // 32 == slot_group)
    hot_i = jnp.where(one_hot_i, 1.0, 0.0)
    j_col = jnp.sum(jnp.where(one_hot_i, lane64 % 32, 0), axis=1, keepdims=True)
    place = block_of(2, slot_group[:, 0:1], j_col) * 16
    flat = q2[:, :, 256:384].reshape(2048, 128)
    wide = iota((64, 2048), 1)
    emb = jnp.concatenate(
        [nn(jnp.where(wide == place + c, 1.0, 0.0).astype(BF16), flat) for c in range(6)], axis=1
    )
    hot_row = jnp.where(iota((64, 64), 1) == row_col, 1.0, 0.0).astype(BF16)
    keys = nn(hot_row, keys_ref[...])
    retrieval = jnp.sum(emb * keys, axis=1, keepdims=True) * (E ** (-0.5))
    square = iota((64, 64), 0) == iota((64, 64), 1)
    retrieval_row = jnp.sum(jnp.where(square, retrieval, 0.0), axis=0, keepdims=True)
    k_row = lane_ref[4:5, 0:64]
    by_k = jnp.where(iota((32, 64), 0) == k_row, retrieval_row, 0.0)
    t2[...] = nn(by_k, hot_i, HIGHEST)

    size = (64, 64, 16)

    def combine(p, values):
        if p == 2:
            total = values[0]
            for value in values[1:]:
                total = total + value
            return total
        top = values[0]
        for value in values[1:]:
            top = jnp.maximum(top, value)
        total = jnp.exp(values[0] - top)
        for value in values[1:]:
            total = total + jnp.exp(value - top)
        return top + jnp.log(total)

    for p in range(3):
        other = pl.ds(pl.multiple_of((1 - core) * size[p], size[p]), size[p])
        start(ts[p].at[other], acs[p], AR + p * 11, sibling)
    for p in range(3):
        own = pl.ds(pl.multiple_of(core * size[p], size[p]), size[p])
        arrived(acs[p], AR + p * 11)
        accs[p][0] = combine(p, [ts[p][own, :], acs[p][...]])
        for step in (1, 2, 3):
            start(
                accs[p].at[0],
                ars[p].at[step - 1],
                AR + p * 11 + step,
                peer(ORDERS[p][0], step),
            )
    for stage in range(3):
        for p in range(3):
            values = [accs[p][stage]]
            for step in (1, 2, 3):
                arrived(ars[p].at[stage * 3 + step - 1], AR + p * 11 + stage * 3 + step)
                values.append(ars[p][stage * 3 + step - 1])
            total = combine(p, values)
            own = pl.ds(pl.multiple_of(core * size[p], size[p]), size[p])
            if stage == 2:
                ls[p][own, :] = total
                ref = ls[p].at[own]
                start(ref, ref, AR + p * 11 + 10, sibling)
            else:
                accs[p][stage + 1] = total
                for step in (1, 2, 3):
                    start(
                        accs[p].at[stage + 1],
                        ars[p].at[(stage + 1) * 3 + step - 1],
                        AR + p * 11 + (stage + 1) * 3 + step,
                        peer(ORDERS[p][stage + 1], step),
                    )
    for p in range(3):
        other = pl.ds(pl.multiple_of((1 - core) * size[p], size[p]), size[p])
        arrived(ls[p].at[other], AR + p * 11 + 10)

    log_sum = jnp.concatenate([l0[...], l1[...]], axis=0)
    targets = []
    for g in range(4):
        chosen = jnp.where(sub == ir_ref[g : g + 1, :], 1.0, 0.0)
        weights = jnp.exp(s_buf[g] - nn(log_sum, chosen, HIGHEST))
        p_buf[g] = weights.astype(BF16)
        mass = jnp.sum(weights, axis=0, keepdims=True)
        own = iota((16, 128), 1) // 8 == iota((16, 128), 0)
        targets.append(jnp.sum(jnp.where(own, mass, 0.0), axis=1, keepdims=True))
    target = jnp.concatenate(targets, axis=0) * (1.0 / 256.0)
    raw = l2[...]
    top = jnp.max(raw, axis=0, keepdims=True)
    log_prob_all = raw - top - jnp.log(jnp.sum(jnp.exp(raw - top), axis=0, keepdims=True))
    hot_k = jnp.where(iota((64, 32), 1) == k_col, 1.0, 0.0)
    log_prob = jnp.sum(
        jnp.where(one_hot_i, nn(hot_k, log_prob_all, HIGHEST), 0.0), axis=1, keepdims=True
    )
    term = jnp.where(valid, target * (jnp.log(target) - log_prob), 0.0)
    loss_row = jnp.sum(jnp.where(one_hot_i, term, 0.0), axis=0, keepdims=True)
    loss_col = jnp.sum(jnp.where(sub == lanes, loss_row, 0.0), axis=1, keepdims=True)
    loss_t[...] = jnp.broadcast_to(loss_col, (128, 128))

    def loss_block(j, carry):
        for g in range(4):
            value = jnp.broadcast_to(loss_t[pl.ds(g * 32 + j, 1), :], (8, 128))
            top_half = value.astype(BF16).astype(F32)
            tile = jnp.concatenate([top_half, value - top_half], axis=0)
            c2[block_of(2, g, j), :, 256:384] = tile.astype(BF16)
        return carry

    lax.fori_loop(0, 32, loss_block, 0)

    keep_low = jnp.broadcast_to(lane < 64, (8, 128))

    def context_of(p, tiles):
        def step(n, carry):
            g, cc = n // tiles, n % tiles
            inner = pl.multiple_of(cc * 128, 128)
            outer = pl.multiple_of(D + (3 * p + cc) * 128, 128)
            slots = pl.ds(pl.multiple_of(g * 128, 128), 128)
            right = jnp.concatenate(
                [kv[slots, pl.ds(outer, 128)], kv[slots, pl.ds(outer + 1024, 128)]], axis=1
            )
            row = ir_ref[pl.ds(g, 1), :] - g * 32
            rows = pl.ds(pl.multiple_of((3 * p + cc) * 32, 32), 32)
            weights = p_buf[g, rows, :]
            for jb in range(2):
                left = []
                for jj in range(16):
                    keep = jnp.where(row == jb * 16 + jj, 1.0, 0.0).astype(BF16)
                    left.append(weights * keep)
                out = nn(jnp.concatenate(left, axis=0), right)
                for jj in range(16):
                    halves = []
                    for half in range(2):
                        cols = slice(half * 128, half * 128 + 128)
                        begin = jj * 32 + half * 8
                        halves.append(
                            jnp.where(
                                keep_low,
                                out[begin : begin + 8, cols],
                                out[begin + 16 : begin + 24, cols],
                            )
                        )
                    tile = jnp.concatenate(halves, axis=0).astype(BF16)
                    cs[p][block_of(p, g, jb * 16 + jj), :, pl.ds(inner, 128)] = tile
            return carry

        lax.fori_loop(0, 4 * tiles, step, 0)

    def swap_start(p):
        start(cs[p].at[pl.ds((1 - core) * 64, 64)], rcs[p], RS + p * 10, sibling)

    def reach(p, stage, to):
        first, second, third = ORDERS[p]
        if stage == 0:
            return core * 64 + to * 16, 16
        if stage == 1:
            return core * 64 + at[third] * 16 + to * 4, 4
        return core * 64 + at[third] * 16 + at[second] * 4 + to, 1

    def scatter_start(p, stage):
        axis = ORDERS[p][2 - stage]
        for step in (1, 2, 3):
            begin, count = reach(p, stage, (at[axis] + step) % 4)
            start(
                cs[p].at[pl.ds(begin, count)],
                rstage[stage][p].at[pl.ds((step - 1) * count, count)],
                RS + p * 10 + 1 + stage * 3 + step - 1,
                peer(axis, step),
            )

    def swap_finish(p):
        arrived(rcs[p], RS + p * 10)

        def step(b, carry):
            _, block = add_blocks(p, [cs[p][core * 64 + b], rcs[p][b]])
            cs[p][core * 64 + b] = block
            return carry

        lax.fori_loop(0, 64, step, 0)

    def scatter_wait(p, stage):
        count = (16, 4, 1)[stage]
        for step in (1, 2, 3):
            arrived(
                rstage[stage][p].at[pl.ds((step - 1) * count, count)],
                RS + p * 10 + 1 + stage * 3 + step - 1,
            )

    def scatter_add(p, stage):
        axis = ORDERS[p][2 - stage]
        begin, count = reach(p, stage, at[axis])
        scatter_wait(p, stage)

        def step(b, carry):
            parts = [rstage[stage][p][n * count + b] for n in range(3)]
            _, block = add_blocks(p, [cs[p][begin + b]] + parts)
            cs[p][begin + b] = block
            return carry

        lax.fori_loop(0, count, step, 0)

    context_of(0, 3)
    swap_start(0)
    context_of(1, 3)
    swap_start(1)
    swap_finish(0)
    scatter_start(0, 0)
    context_of(2, 2)
    swap_start(2)
    swap_finish(1)
    scatter_start(1, 0)
    swap_finish(2)
    scatter_start(2, 0)

    coefficient = (LOSS_WEIGHT * E ** (-0.5)) * (jnp.exp(log_prob) - target)
    grads = jnp.where(valid, coefficient * emb, 0.0).astype(BF16)
    hot_row_t = jnp.where(iota((64, 64), 0) == lane_ref[5:6, 0:64], 1.0, 0.0).astype(BF16)
    grad_ref[...] = nn(hot_row_t, grads)

    for p in range(3):
        scatter_add(p, 0)
        scatter_start(p, 1)
    for p in range(3):
        scatter_add(p, 1)
        scatter_start(p, 2)
    for p in range(3):
        begin, _ = reach(p, 2, at[ORDERS[p][0]])
        scatter_wait(p, 2)
        total, _ = add_blocks(p, [cs[p][begin]] + [rstage[2][p][n] for n in range(3)])
        for cc in range(2 if p == 2 else 3):
            c = 3 * p + cc
            cols = total[:, cc * 128 : cc * 128 + 128].astype(BF16)
            ctx_ref[0, :, c * 128 : c * 128 + 128] = total[0:8, cc * 128 : cc * 128 + 128].astype(BF16)
            ctx_ref[0, :, 1024 + c * 128 : 1152 + c * 128] = total[
                8:16, cc * 128 : cc * 128 + 128
            ].astype(BF16)
        if p == 2:
            loss_ref[...] = total[0:8, 256:384] + total[8:16, 256:384]

    for copy in started:
        copy.wait_send()


def body(
    store_states,
    store_keys,
    passage_ids,
    store_slot,
    row_question,
    queries,
    question_emb,
    enc_gain,
    key_weight,
    value_weight,
):
    me = lax.axis_index("group") * lax.axis_size("dev") + lax.axis_index("dev")
    rows = store_slot[passage_ids].reshape(GROUPS, 1024)
    mine = rows // STORE == me
    earlier = iota((1024, 1024), 0) <= iota((1024, 1024), 1)
    rank = jnp.dot(mine.astype(BF16), earlier.astype(BF16), preferred_element_type=F32)
    rank = rank.astype(jnp.int32) - 1
    hit = mine[:, None, :] & (rank[:, None, :] == jnp.arange(SLOTS)[None, :, None])
    code = iota((GROUPS, 1024), 1) * STORE + rows % STORE + 1
    code = jnp.sum(jnp.where(hit, code[:, None, :], 0), axis=2).reshape(64) - 1
    valid = code >= 0
    u = jnp.where(valid, code // (32 * STORE), -1)
    k = jnp.where(valid, (code // STORE) % 32, 0)
    row = jnp.where(valid, code % STORE, -1)
    rows_of = jnp.maximum(row, 0)
    u_lanes = jnp.repeat(u.reshape(4, 16), 8, axis=1)
    pad = jnp.zeros((64,), jnp.int32)
    lane_tab = jnp.concatenate(
        [
            u_lanes,
            jnp.concatenate([k, pad])[None],
            jnp.concatenate([row, pad])[None],
            jnp.zeros((2, 128), jnp.int32),
        ]
    )
    col_tab = jnp.pad(jnp.stack([u, k, row], axis=1), ((0, 0), (0, 125)))
    rq = row_question[0]
    rq_tab = jnp.concatenate(
        [
            jnp.broadcast_to(rq[:, None], (32, 128)),
            jnp.broadcast_to(jnp.tile(rq, 4)[None, :], (8, 128)),
        ]
    )
    vmem = pl.BlockSpec(memory_space=pltpu.VMEM)
    anywhere = pl.BlockSpec(memory_space=pl.ANY)
    scratch = [
        pltpu.VMEM((64, 8, D), BF16),
        pltpu.VMEM((D, 2 * D), BF16),
        pltpu.VMEM((512, D), BF16),
        pltpu.VMEM((512, 2 * D), BF16),
    ]
    scratch += [pltpu.VMEM((128, 16, 384), BF16)] * 6
    scratch += [pltpu.VMEM((64, 16, 384), BF16)] * 3
    scratch += [pltpu.VMEM((48, 16, 384), BF16)] * 3
    scratch += [pltpu.VMEM((12, 16, 384), BF16)] * 3
    scratch += [pltpu.VMEM((3, 16, 384), BF16)] * 3
    scratch += [pltpu.VMEM((4, 256, 128), F32), pltpu.VMEM((4, 256, 128), BF16)]
    sizes = (64, 64, 16)
    scratch += [pltpu.VMEM((2 * n, 128), F32) for n in sizes]
    scratch += [pltpu.VMEM((n, 128), F32) for n in sizes]
    scratch += [pltpu.VMEM((9, n, 128), F32) for n in sizes]
    scratch += [pltpu.VMEM((3, n, 128), F32) for n in sizes]
    scratch += [pltpu.VMEM((2 * n, 128), F32) for n in sizes]
    scratch += [
        pltpu.VMEM((4, 40, 128), jnp.int32),
        pltpu.VMEM((8, 128), jnp.int32),
        pltpu.VMEM((128, 128), F32),
        pltpu.SemaphoreType.DMA((SEMS,)),
        pltpu.SemaphoreType.DMA((SEMS,)),
        pltpu.SemaphoreType.DMA((9,)),
    ]
    context, loss, grad = pl.pallas_call(
        kernel,
        out_shape=(
            jax.ShapeDtypeStruct((1, 8, D), BF16),
            jax.ShapeDtypeStruct((8, 128), F32),
            jax.ShapeDtypeStruct((STORE, E), F32),
        ),
        in_specs=[
            pl.BlockSpec(memory_space=pltpu.SMEM),
            vmem,
            vmem,
            vmem,
            anywhere,
            vmem,
            vmem,
            vmem,
            vmem,
            anywhere,
            anywhere,
        ],
        out_specs=(vmem, vmem, vmem),
        scratch_shapes=scratch,
        compiler_params=pltpu.CompilerParams(
            collective_id=0, has_side_effects=True, vmem_limit_bytes=60 * 1024 * 1024
        ),
        cost_estimate=pl.CostEstimate(
            flops=12 * 10**9, bytes_accessed=20 * 10**6, transcendentals=10**6
        ),
    )(
        rows_of,
        lane_tab,
        col_tab,
        rq_tab,
        store_states,
        store_keys,
        queries,
        question_emb,
        enc_gain.reshape(1, D),
        key_weight,
        value_weight,
    )
    return context, loss[0, 0:1], grad


def solution(mesh):
    in_specs = (
        P(("group", "dev"), None, None),
        P(("group", "dev"), None),
        P(),
        P(),
        P("group", None),
        P(("group", "dev"), None, None),
        P(("group", "dev"), None),
        P(),
        P(),
        P(),
    )
    out_specs = (P(("group", "dev"), None, None), P(("group", "dev")), P(("group", "dev"), None))
    return jax.shard_map(body, mesh=mesh, in_specs=in_specs, out_specs=out_specs, check_vma=False)
```

time: 277 us -> 129 us (0.47)
  waiting for transfers between devices: 129 us -> 0 us
  Pallas kernels: 0 us -> 94.3 us
  starting transfers between devices: 53.3 us -> 0 us
  local copies, waits for them, and re-layouts: 60.9 us -> 29.9 us
  matrix products: 24.6 us -> 0.31 us
  other arithmetic: 6.4 us -> 2.88 us
    all_to_all x7 -> x0, waiting for transfers between devices: 129 us -> none  [the longest x1 94.4 us: body(): lax.all_to_all(store_states[send_local], ('group', 'dev'), split_axis=0,...]
    pallas_call x0 -> x1, Pallas kernels: none -> 94.3 us  [body(): pl.pallas_call(kernel, out_shape=(jax.ShapeDtypeStruct((1, 8, D), BF16),...]
    all_to_all x7 -> x0, starting transfers between devices: 53.3 us -> none  [the longest x1 11.1 us: body(): lax.all_to_all(store_keys[send_local], ('group', 'dev'), split_axis=0, co...]
    dot_general x7 -> x1, matrix products: 24.6 us -> 0.31 us  [body(): jnp.dot(mine.astype(BF16), earlier.astype(BF16), preferred_element_type=F32)]
    gather x9 -> x1, local copies, waits for them, and re-layouts: 44.4 us -> 23 us  [body(): rows = store_slot[passage_ids].reshape(GROUPS, 1024)]
    another operation x2, local copies, waits for them, and re-layouts: 6.4 us -> 0.75 us  [the longest x1 0.66 us: body(): jnp.tile(rq, 4)[None, :]]
  transfers between devices with their start and end apart: 7 -> 0, of which waited for: 5 -> 0; matrix products, arithmetic and copies ran while one was open for 18% -> 0% of each run, Pallas kernels for 0% -> 0%
where the time goes in v1:
time: 129 us; the launch traced here: 128 us
  Pallas kernels  94.3 us (73%)
  local copies, waits for them, and re-layouts  29.9 us (23%)
  other arithmetic  2.88 us (2%)
    pallas_call x1, Pallas kernels, body(): pl.pallas_call(kernel, out_shape=(jax.ShapeDtypeStruct((1, 8, D), BF16),...  94.3 us
    gather x1, local copies, waits for them, and re-layouts, body(): rows = store_slot[passage_ids].reshape(GROUPS, 1024)  23 us
    unnamed x4, local copies, waits for them, and re-layouts  3 us

profile of v1, /device:TPU:0, one launch (start us, length us, event | category | flops | bytes accessed | tf_op | source)
XLA Modules:
  0.0 128.2 jit_solution(12386844993977741581)
XLA Ops:
  0.6 0.0 copy-start
  0.7 0.7 pad.7.clone
  1.3 0.1 pad.15.clone
  1.4 0.7 tile.2
  2.0 0.1 broadcast_in_dim.58
  2.1 0.7 pad_add_fusion.own_rq_ref
  2.8 0.7 compare_select_fusion
  3.5 0.1 copy.26
  3.6 0.1 reshape.247
  3.7 0.0 copy-done
  3.7 23.0 %gather_fusion = s32[4096]{0:T(1024)S(1)} fusion(s32[8192]{0:T(1024)S(1)} %copy-done, s32[4096]{0:T(1024)S(1)} %broadcast_clamp_fusion), kind=kCustom, calls=%fused_computation | custom fusion | bytes 49152 | tf_op jit(solution)/shard_map/gather | solution.py:627
  26.9 0.3 fusion.2
  27.2 0.2 select_reduce_fusion
  27.4 0.1 sub.37
  27.5 0.1 sub.34
  27.6 0.5 broadcast_maximum_fusion
  28.1 0.1 copy.27
  28.2 0.6 pad.6.col_ref
  28.8 0.1 broadcast_in_dim.52
  28.9 0.1 reshape.243
  29.0 0.7 add_add_fusion.lane_ref
  29.7 94.3 %shard_map.121 = (bf16[1,8,2048]{2,1,0:T(8,128)(2,1)}, f32[8,128]{1,0:T(8,128)}, f32[64,768]{1,0:T(8,128)}) custom-call(s32[64]{0:T(128)} %get-tuple-element.9.rows_ref, s32[8,128]{1,0:T(8,128)} %add_add_fusion.lane_ref, s32[64,128]{1,0:T(8,128)} %pad.6.col_ref, s32[40,128]{1,0:T(8,128)} %pad_add_fusion.own_rq_ref, bf16[64,8,2048]{2,1,0:T(8,128)(2,1)} %states_ref.1, ...), custom_call_target="tpu_custom_call" | custom-call | flops 12000000000 | bytes 20000000 | tf_op jit(solution)/shard_map/pallas_call | solution.py:686
  124.0 1.2 slice.3
  125.2 1.4 %copy.30 = bf16[1,8,2048]{2,1,0:T(8,128)(2,1)} copy(bf16[1,8,2048]{2,1,0:T(8,128)(2,1)} %get-tuple-element.22) | data formatting | bytes 65536
  126.5 1.6 %copy.31 = f32[64,768]{1,0:T(8,128)} copy(f32[64,768]{1,0:T(8,128)} %get-tuple-element.24) | data formatting | bytes 393216
  (11 shorter events, 0.1 us)
Async XLA Ops:
  0.6 3.1 %copy-start = (s32[8192]{0:T(1024)S(1)}, s32[8192]{0:T(1024)}, u32[]{:S(2)}) copy-start(s32[8192]{0:T(1024)} %param.13) | copy-start | bytes 98308

commit v2 on v1

--- a/solution.py
+++ b/solution.py
@@ -62,10 +62,9 @@
 
 
 def kernel(
-    rows_ref,
-    lane_ref,
-    col_ref,
-    own_rq_ref,
+    ids_ref,
+    slot_ref,
+    rq_ref,
     states_ref,
     keys_ref,
     queries_ref,
@@ -78,6 +77,8 @@
     grad_ref,
     st,
     w,
+    stored,
+    pick,
     nrm,
     kv,
     q0,
@@ -116,6 +117,7 @@
     l1,
     l2,
     rqt,
+    lane_ref,
     ir_ref,
     loss_t,
     send_sem,
@@ -195,7 +197,9 @@
     emb_rows = [emb_ref[:, c * 128 : c * 128 + 128].astype(F32) for c in range(6)]
     emb_tile = jnp.concatenate(emb_rows + [jnp.zeros((10, 128), F32)], axis=0)
     q2[mine[2], :, 256:384] = emb_tile.astype(BF16)
-    rqt[my_group] = own_rq_ref[...]
+    diagonal = iota((32, 32), 0) == iota((32, 32), 1)
+    rq_col = jnp.sum(jnp.where(diagonal, rq_ref[...], 0), axis=1, keepdims=True)
+    rqt[my_group] = jnp.broadcast_to(rq_col, (32, 128))
 
     barrier = pltpu.get_barrier_semaphore()
     pl.semaphore_signal(barrier, inc=1, device_id=sibling, device_id_type=MESH)
@@ -231,20 +235,80 @@
 
     gather_start(0)
     for step in (1, 2, 3):
-        start(own_rq_ref, rqt.at[my_group], RQ + step - 1, peer("z", step))
+        start(rqt.at[my_group], rqt.at[my_group], RQ + step - 1, peer("z", step))
+
+    lane = iota((1, 128), 1)
+    sub = iota((128, 128), 0)
+    lanes = iota((128, 128), 1)
+    first_row = (my_group * PER_GROUP + my_dev) * STORE
+    local = slot_ref[...] - first_row
+    local = jnp.where((local >= 0) & (local < STORE), local + 1, 0).astype(F32)
+    local_t = jnp.transpose(local).astype(BF16)
+    ids_high = ids_ref[...] // 128
+    ids_low = ids_ref[...] % 128
+    high_sub = iota((64, 128), 0)
+    lane32 = iota((128, 32), 1)
+    held_rows = []
+    for k in range(32):
+        hot = jnp.where(high_sub == ids_high[k : k + 1, :], 1.0, 0.0).astype(BF16)
+        found = jnp.where(sub == ids_low[k : k + 1, :], nn(local_t, hot), 0.0)
+        held_rows.append(jnp.sum(found, axis=0, keepdims=True))
+    held = jnp.transpose(jnp.concatenate(held_rows, axis=0))
+    held_int = held.astype(jnp.int32)
+    mine_f = jnp.where(held_int > 0, 1.0, 0.0)
+    mine_b = mine_f.astype(BF16)
+    in_row = nn(mine_b, jnp.ones((32, 32), BF16))
+    above = jnp.where((sub // 32 == lanes // 32) & (lanes < sub), 1.0, 0.0).astype(BF16)
+    upto = jnp.where(iota((32, 32), 0) <= iota((32, 32), 1), 1.0, 0.0).astype(BF16)
+    rank = nn(above, in_row.astype(BF16)) + nn(mine_b, upto)
+    rank = jnp.where(held_int > 0, rank.astype(jnp.int32), 0)
+    code = (iota((128, 32), 0) % 32) * 4096 + lane32 * 128 + held_int
+    spread = jnp.zeros((128, 128), jnp.int32)
+    for n in range(SLOTS):
+        here = jnp.sum(jnp.where(rank == n + 1, code, 0), axis=1, keepdims=True)
+        spread = jnp.where(lanes // 8 == n, here, spread)
+    code_cols = []
+    slot16 = iota((16, 128), 1) == iota((16, 128), 0) * 8
+    for g in range(4):
+        code_row = jnp.sum(spread[g * 32 : g * 32 + 32], axis=0, keepdims=True)
+        lane_ref[g : g + 1, :] = jnp.where(code_row > 0, code_row // 4096, -1)
+        code_cols.append(jnp.sum(jnp.where(slot16, code_row, 0), axis=1, keepdims=True))
+        long_col = jnp.sum(jnp.where(sub == lanes, code_row, 0), axis=1, keepdims=True)
+        token = jnp.where(
+            long_col > 0, (long_col % 128 - 1) * 8 + iota((128, 1), 0) % 8, 512
+        )
+        pick[g * 128 : g * 128 + 128, :] = jnp.where(
+            iota((128, 512), 1) == token, 1.0, 0.0
+        ).astype(BF16)
+    code_col = jnp.concatenate(code_cols, axis=0)
+    valid = code_col > 0
+    k_col = (code_col // 128) % 32
+    row_col = code_col % 128 - 1
+    square = iota((64, 64), 0) == iota((64, 64), 1)
+    code_row64 = jnp.sum(jnp.where(square, code_col, 0), axis=0, keepdims=True)
+    k_row = (code_row64 // 128) % 32
+    row_row = code_row64 % 128 - 1
 
     states_copy.wait()
 
     def norm_pair(pair, carry):
         both = []
         for half in range(2):
-            values = st[rows_ref[pair * 2 + half]].astype(F32)
+            values = st[pair * 2 + half].astype(F32)
             mean_square = jnp.mean(values * values, axis=-1, keepdims=True)
             both.append(values * lax.rsqrt(mean_square + EPS) * gain_ref[...])
-        nrm[pl.ds(pl.multiple_of(pair * 16, 16), 16), :] = jnp.concatenate(both, axis=0).astype(BF16)
+        rows = pl.ds(pl.multiple_of(pair * 16, 16), 16)
+        stored[rows, :] = jnp.concatenate(both, axis=0).astype(BF16)
         return carry
 
     lax.fori_loop(0, 32, norm_pair, 0)
+
+    def pick_step(n, carry):
+        cols = pl.ds(pl.multiple_of(n * 256, 256), 256)
+        nrm[:, cols] = nn(pick[...], stored[:, cols]).astype(BF16)
+        return carry
+
+    lax.fori_loop(0, 8, pick_step, 0)
 
     def project(begin, end):
         def step(n, carry):
@@ -277,7 +341,7 @@
     for step in (1, 2, 3):
         arrived(rqt.at[(my_group + 4 - step) % 4], RQ + step - 1)
     for g in range(4):
-        match = rqt[g, 0:32, :] == lane_ref[g : g + 1, :]
+        match = rqt[g] == lane_ref[g : g + 1, :]
         row = jnp.sum(jnp.where(match, iota((32, 128), 0) + (g * 32 + 1), 0), axis=0, keepdims=True)
         ir_ref[g : g + 1, :] = row - 1
 
@@ -287,7 +351,6 @@
             begin = (1 - core) * 64 + ((at[third] + 4 - back) % 4) * 16
             arrived(qs[p].at[pl.ds(begin, 16)], AG_SIB + p * 4 + back)
 
-    lane = iota((1, 128), 1)
     low = (lane < 64).astype(F32).astype(BF16)
     high = (lane >= 64).astype(F32).astype(BF16)
 
@@ -325,8 +388,6 @@
     scores_of(1, 3)
     scores_of(2, 2)
 
-    sub = iota((128, 128), 0)
-    lanes = iota((128, 128), 1)
     peak_i = jnp.zeros((256, 128), F32)
     total_i = jnp.zeros((256, 128), F32)
     present = jnp.zeros((8, 128), F32)
@@ -364,19 +425,16 @@
     t0[...] = table[0:128, :]
     t1[...] = table[128:256, :]
 
-    u_col = jnp.concatenate([col_ref[:, 0:1]], axis=0)
-    k_col = col_ref[:, 1:2]
-    row_col = col_ref[:, 2:3]
-    valid = u_col >= 0
     lane64 = iota((64, 128), 1)
-    slot_group = iota((64, 128), 0) // 16
-    row_question = jnp.concatenate(
-        [jnp.broadcast_to(rqt[g, 32:33, :], (16, 128)) for g in range(4)], axis=0
-    )
-    one_hot_i = (row_question == u_col) & (lane64 // 32 == slot_group)
+    i_cols = []
+    for g in range(4):
+        picked = jnp.where(slot16, ir_ref[g : g + 1, :] + 1, 0)
+        i_cols.append(jnp.sum(picked, axis=1, keepdims=True))
+    i_col = jnp.concatenate(i_cols, axis=0) - 1
+    one_hot_i = lane64 == i_col
     hot_i = jnp.where(one_hot_i, 1.0, 0.0)
-    j_col = jnp.sum(jnp.where(one_hot_i, lane64 % 32, 0), axis=1, keepdims=True)
-    place = block_of(2, slot_group[:, 0:1], j_col) * 16
+    decoder = jnp.maximum(i_col, 0)
+    place = block_of(2, decoder // 32, decoder % 32) * 16
     flat = q2[:, :, 256:384].reshape(2048, 128)
     wide = iota((64, 2048), 1)
     emb = jnp.concatenate(
@@ -385,9 +443,7 @@
     hot_row = jnp.where(iota((64, 64), 1) == row_col, 1.0, 0.0).astype(BF16)
     keys = nn(hot_row, keys_ref[...])
     retrieval = jnp.sum(emb * keys, axis=1, keepdims=True) * (E ** (-0.5))
-    square = iota((64, 64), 0) == iota((64, 64), 1)
     retrieval_row = jnp.sum(jnp.where(square, retrieval, 0.0), axis=0, keepdims=True)
-    k_row = lane_ref[4:5, 0:64]
     by_k = jnp.where(iota((32, 64), 0) == k_row, retrieval_row, 0.0)
     t2[...] = nn(by_k, hot_i, HIGHEST)
 
@@ -584,7 +640,7 @@
 
     coefficient = (LOSS_WEIGHT * E ** (-0.5)) * (jnp.exp(log_prob) - target)
     grads = jnp.where(valid, coefficient * emb, 0.0).astype(BF16)
-    hot_row_t = jnp.where(iota((64, 64), 0) == lane_ref[5:6, 0:64], 1.0, 0.0).astype(BF16)
+    hot_row_t = jnp.where(iota((64, 64), 0) == row_row, 1.0, 0.0).astype(BF16)
     grad_ref[...] = nn(hot_row_t, grads)
 
     for p in range(3):
@@ -611,6 +667,12 @@
         copy.wait_send()
 
 
+def hand_over(ctx_ref, loss_ref, grad_ref, ctx_out, loss_out, grad_out):
+    ctx_out[...] = ctx_ref[...]
+    loss_out[0] = loss_ref[0, 0]
+    grad_out[...] = grad_ref[...]
+
+
 def body(
     store_states,
     store_keys,
@@ -623,43 +685,13 @@
     key_weight,
     value_weight,
 ):
-    me = lax.axis_index("group") * lax.axis_size("dev") + lax.axis_index("dev")
-    rows = store_slot[passage_ids].reshape(GROUPS, 1024)
-    mine = rows // STORE == me
-    earlier = iota((1024, 1024), 0) <= iota((1024, 1024), 1)
-    rank = jnp.dot(mine.astype(BF16), earlier.astype(BF16), preferred_element_type=F32)
-    rank = rank.astype(jnp.int32) - 1
-    hit = mine[:, None, :] & (rank[:, None, :] == jnp.arange(SLOTS)[None, :, None])
-    code = iota((GROUPS, 1024), 1) * STORE + rows % STORE + 1
-    code = jnp.sum(jnp.where(hit, code[:, None, :], 0), axis=2).reshape(64) - 1
-    valid = code >= 0
-    u = jnp.where(valid, code // (32 * STORE), -1)
-    k = jnp.where(valid, (code // STORE) % 32, 0)
-    row = jnp.where(valid, code % STORE, -1)
-    rows_of = jnp.maximum(row, 0)
-    u_lanes = jnp.repeat(u.reshape(4, 16), 8, axis=1)
-    pad = jnp.zeros((64,), jnp.int32)
-    lane_tab = jnp.concatenate(
-        [
-            u_lanes,
-            jnp.concatenate([k, pad])[None],
-            jnp.concatenate([row, pad])[None],
-            jnp.zeros((2, 128), jnp.int32),
-        ]
-    )
-    col_tab = jnp.pad(jnp.stack([u, k, row], axis=1), ((0, 0), (0, 125)))
-    rq = row_question[0]
-    rq_tab = jnp.concatenate(
-        [
-            jnp.broadcast_to(rq[:, None], (32, 128)),
-            jnp.broadcast_to(jnp.tile(rq, 4)[None, :], (8, 128)),
-        ]
-    )
     vmem = pl.BlockSpec(memory_space=pltpu.VMEM)
     anywhere = pl.BlockSpec(memory_space=pl.ANY)
     scratch = [
         pltpu.VMEM((64, 8, D), BF16),
         pltpu.VMEM((D, 2 * D), BF16),
+        pltpu.VMEM((512, D), BF16),
+        pltpu.VMEM((512, 512), BF16),
         pltpu.VMEM((512, D), BF16),
         pltpu.VMEM((512, 2 * D), BF16),
     ]
@@ -676,7 +708,8 @@
     scratch += [pltpu.VMEM((3, n, 128), F32) for n in sizes]
     scratch += [pltpu.VMEM((2 * n, 128), F32) for n in sizes]
     scratch += [
-        pltpu.VMEM((4, 40, 128), jnp.int32),
+        pltpu.VMEM((4, 32, 128), jnp.int32),
+        pltpu.VMEM((8, 128), jnp.int32),
         pltpu.VMEM((8, 128), jnp.int32),
         pltpu.VMEM((128, 128), F32),
         pltpu.SemaphoreType.DMA((SEMS,)),
@@ -691,7 +724,6 @@
             jax.ShapeDtypeStruct((STORE, E), F32),
         ),
         in_specs=[
-            pl.BlockSpec(memory_space=pltpu.SMEM),
             vmem,
             vmem,
             vmem,
@@ -712,10 +744,9 @@
             flops=12 * 10**9, bytes_accessed=20 * 10**6, transcendentals=10**6
         ),
     )(
-        rows_of,
-        lane_tab,
-        col_tab,
-        rq_tab,
+        passage_ids.T,
+        store_slot.reshape(64, 128),
+        row_question,
         store_states,
         store_keys,
         queries,
@@ -724,7 +755,16 @@
         key_weight,
         value_weight,
     )
-    return context, loss[0, 0:1], grad
+    return pl.pallas_call(
+        hand_over,
+        out_shape=(
+            jax.ShapeDtypeStruct((1, 8, D), BF16),
+            jax.ShapeDtypeStruct((1,), F32),
+            jax.ShapeDtypeStruct((STORE, E), F32),
+        ),
+        in_specs=[vmem, vmem, vmem],
+        out_specs=(vmem, pl.BlockSpec(memory_space=pltpu.SMEM), vmem),
+    )(context, loss, grad)
 
 
 def solution(mesh):

time: 129 us -> 101 us (0.78)
  local copies, waits for them, and re-layouts: 29.9 us -> 0 us
  Pallas kernels: 94.3 us -> 100 us
  other arithmetic: 2.88 us -> 0 us
    gather x1 -> x0, local copies, waits for them, and re-layouts: 23 us -> none  [body(): rows = store_slot[passage_ids].reshape(GROUPS, 1024)]
    pallas_call x1, Pallas kernels: 94.3 us -> 98.7 us  [body(): pl.pallas_call(kernel, out_shape=(jax.ShapeDtypeStruct((1, 8, D), BF16),...]
    unnamed x4 -> x0, local copies, waits for them, and re-layouts: 3 us -> none
    pallas_call x0 -> x1, Pallas kernels: none -> 1.65 us  [body(): pl.pallas_call(hand_over, out_shape=(jax.ShapeDtypeStruct((1, 8, D), BF16...]
    concatenate x2 -> x0, other arithmetic: 1.35 us -> none  [the longest x1 0.68 us: body(): jnp.concatenate([jnp.broadcast_to(rq[:, None], (32, 128)), jnp.broadcast_...]
where the time goes in v2:
time: 101 us
  Pallas kernels  100 us (99%)
    pallas_call x1, Pallas kernels, body(): pl.pallas_call(kernel, out_shape=(jax.ShapeDtypeStruct((1, 8, D), BF16),...  98.7 us

profile of v2, /device:TPU:0, one launch (start us, length us, event | category | flops | bytes accessed | tf_op | source)
XLA Modules:
  0.0 101.0 jit_solution(536509305469190870)
XLA Ops:
  0.6 98.7 %shard_map.121 = (bf16[1,8,2048]{2,1,0:T(8,128)(2,1)}, f32[8,128]{1,0:T(8,128)}, f32[64,768]{1,0:T(8,128)}) custom-call(s32[32,128]{1,0:T(8,128)} %bitcast.4, s32[64,128]{1,0:T(8,128)} %bitcast.3, s32[1,32]{1,0:T(1,128)} %rq_ref.1, bf16[64,8,2048]{2,1,0:T(8,128)(2,1)} %states_ref.1, bf16[64,768]{1,0:T(8,128)(2,1)} %keys_ref.1, ...), custom_call_target="tpu_custom_call" | custom-call | flops 12000000000 | bytes 20000000 | tf_op jit(solution)/shard_map/pallas_call | solution.py:719
  99.3 1.7 %shard_map.122 = (bf16[1,8,2048]{2,1,0:T(8,128)(2,1)}, f32[1]{0:T(128)}, f32[64,768]{1,0:T(8,128)}) custom-call(bf16[1,8,2048]{2,1,0:T(8,128)(2,1)} %get-tuple-element.6.ctx_ref, f32[8,128]{1,0:T(8,128)} %get-tuple-element.7.loss_ref, f32[64,768]{1,0:T(8,128)} %get-tuple-element.8.grad_ref), custom_call_target="tpu_custom_call" | custom-call | tf_op jit(solution)/shard_map/pallas_call | solution.py:758

commit v3 on v2

--- a/solution.py
+++ b/solution.py
@@ -25,7 +25,7 @@
 
 ORDERS = (("x", "y", "z"), ("y", "z", "x"), ("z", "x", "y"))
 AG, AG_SIB, RQ, AR, RS = 0, 27, 39, 42, 75
-SEMS = 105
+SEMS = 114
 
 
 def nt(a, b, precision=None):
@@ -119,6 +119,8 @@
     rqt,
     lane_ref,
     ir_ref,
+    block_ref,
+    block_smem,
     loss_t,
     send_sem,
     recv_sem,
@@ -254,6 +256,11 @@
         found = jnp.where(sub == ids_low[k : k + 1, :], nn(local_t, hot), 0.0)
         held_rows.append(jnp.sum(found, axis=0, keepdims=True))
     held = jnp.transpose(jnp.concatenate(held_rows, axis=0))
+    for p in range(3):
+        for step in (1, 2, 3):
+            gather_wait(p, 0, step)
+    gather_start(1)
+
     held_int = held.astype(jnp.int32)
     mine_f = jnp.where(held_int > 0, 1.0, 0.0)
     mine_b = mine_f.astype(BF16)
@@ -303,40 +310,12 @@
 
     lax.fori_loop(0, 32, norm_pair, 0)
 
-    def pick_step(n, carry):
-        cols = pl.ds(pl.multiple_of(n * 256, 256), 256)
-        nrm[:, cols] = nn(pick[...], stored[:, cols]).astype(BF16)
-        return carry
-
-    lax.fori_loop(0, 8, pick_step, 0)
-
-    def project(begin, end):
-        def step(n, carry):
-            offset = pl.multiple_of(n * 256, 256)
-            kv[:, pl.ds(offset, 256)] = nn(nrm[...], w[:, pl.ds(offset, 256)]).astype(BF16)
-            return carry
-
-        for n in range(begin, end):
-            w_copies[n].wait()
-        lax.fori_loop(begin * 2, end * 2, step, 0)
-
-    for p in range(3):
-        for step in (1, 2, 3):
-            gather_wait(p, 0, step)
-    gather_start(1)
-    project(0, 2)
     for p in range(3):
         for step in (1, 2, 3):
             gather_wait(p, 1, step)
     gather_start(2)
     for p in range(3):
         forward(p, 0)
-    project(2, 6)
-    for step in (1, 3, 2):
-        for p in range(3):
-            gather_wait(p, 2, step)
-            forward(p, step)
-    project(6, 8)
 
     for step in (1, 2, 3):
         arrived(rqt.at[(my_group + 4 - step) % 4], RQ + step - 1)
@@ -344,6 +323,36 @@
         match = rqt[g] == lane_ref[g : g + 1, :]
         row = jnp.sum(jnp.where(match, iota((32, 128), 0) + (g * 32 + 1), 0), axis=0, keepdims=True)
         ir_ref[g : g + 1, :] = row - 1
+    decoder_of = jnp.maximum(ir_ref[0:4, :], 0)
+    for p in range(3):
+        block_ref[p * 4 : p * 4 + 4, :] = block_of(p, decoder_of // 32, decoder_of % 32)
+    block_copy = pltpu.make_async_copy(block_ref, block_smem, local_sem.at[9])
+    block_copy.start()
+
+    def pick_step(n, carry):
+        cols = pl.ds(pl.multiple_of(n * 256, 256), 256)
+        nrm[:, cols] = nn(pick[...], stored[:, cols]).astype(BF16)
+        return carry
+
+    lax.fori_loop(0, 8, pick_step, 0)
+
+    def project(begin, end):
+        def step(n, carry):
+            offset = pl.multiple_of(n * 256, 256)
+            kv[:, pl.ds(offset, 256)] = nn(nrm[...], w[:, pl.ds(offset, 256)]).astype(BF16)
+            return carry
+
+        for n in range(begin, end):
+            w_copies[n].wait()
+        lax.fori_loop(begin * 2, end * 2, step, 0)
+
+    project(0, 6)
+    for step in (1, 3, 2):
+        for p in range(3):
+            gather_wait(p, 2, step)
+            forward(p, step)
+    project(6, 8)
+    block_copy.wait()
 
     for p in range(3):
         for back in range(4):
@@ -363,21 +372,19 @@
             right = jnp.concatenate(
                 [kv[slots, pl.ds(outer, 128)], kv[slots, pl.ds(outer + 1024, 128)]], axis=0
             )
-            row = ir_ref[pl.ds(g, 1), :] - g * 32
+            left = []
+            for r in range(SLOTS):
+                block = qs[p][block_smem[p * 4 + g, r * 8], :, pl.ds(inner, 128)]
+                left += [block * low, block * high]
+            out = nt(jnp.concatenate(left, axis=0), right)
             total = [jnp.zeros((8, 128), F32) for _ in range(4)]
-            for jb in range(2):
-                left = []
-                for jj in range(16):
-                    block = qs[p][block_of(p, g, jb * 16 + jj), :, pl.ds(inner, 128)]
-                    left += [block * low, block * high]
-                out = nt(jnp.concatenate(left, axis=0), right)
-                for jj in range(16):
-                    keep = jnp.broadcast_to(row == jb * 16 + jj, (8, 128))
-                    for tile in range(4):
-                        half = tile % 2
-                        begin = jj * 32 + tile * 8
-                        piece = out[begin : begin + 8, half * 128 : half * 128 + 128]
-                        total[tile] = jnp.where(keep, piece, total[tile])
+            for r in range(SLOTS):
+                keep = jnp.broadcast_to(lane // 8 == r, (8, 128))
+                for tile in range(4):
+                    half = tile % 2
+                    begin = r * 32 + tile * 8
+                    piece = out[begin : begin + 8, half * 128 : half * 128 + 128]
+                    total[tile] = jnp.where(keep, piece, total[tile])
             rows = pl.ds(pl.multiple_of((3 * p + cc) * 32, 32), 32)
             s_buf[g, rows, :] = jnp.concatenate(total, axis=0) * (64 ** (-0.5))
             return carry
@@ -536,9 +543,10 @@
 
     keep_low = jnp.broadcast_to(lane < 64, (8, 128))
 
-    def context_of(p, tiles):
-        def step(n, carry):
-            g, cc = n // tiles, n % tiles
+    def context_set(p, to):
+        tiles = 2 if p == 2 else 3
+
+        def tile_of(g, cc, decoders):
             inner = pl.multiple_of(cc * 128, 128)
             outer = pl.multiple_of(D + (3 * p + cc) * 128, 128)
             slots = pl.ds(pl.multiple_of(g * 128, 128), 128)
@@ -548,17 +556,18 @@
             row = ir_ref[pl.ds(g, 1), :] - g * 32
             rows = pl.ds(pl.multiple_of((3 * p + cc) * 32, 32), 32)
             weights = p_buf[g, rows, :]
-            for jb in range(2):
+            for first in range(0, len(decoders), 16):
+                batch = decoders[first : first + 16]
                 left = []
-                for jj in range(16):
-                    keep = jnp.where(row == jb * 16 + jj, 1.0, 0.0).astype(BF16)
+                for j in batch:
+                    keep = jnp.where(row == j, 1.0, 0.0).astype(BF16)
                     left.append(weights * keep)
                 out = nn(jnp.concatenate(left, axis=0), right)
-                for jj in range(16):
+                for n, j in enumerate(batch):
                     halves = []
                     for half in range(2):
                         cols = slice(half * 128, half * 128 + 128)
-                        begin = jj * 32 + half * 8
+                        begin = n * 32 + half * 8
                         halves.append(
                             jnp.where(
                                 keep_low,
@@ -567,13 +576,26 @@
                             )
                         )
                     tile = jnp.concatenate(halves, axis=0).astype(BF16)
-                    cs[p][block_of(p, g, jb * 16 + jj), :, pl.ds(inner, 128)] = tile
-            return carry
-
-        lax.fori_loop(0, 4 * tiles, step, 0)
-
-    def swap_start(p):
-        start(cs[p].at[pl.ds((1 - core) * 64, 64)], rcs[p], RS + p * 10, sibling)
+                    cs[p][block_of(p, g, j), :, pl.ds(inner, 128)] = tile
+
+        if p == 0:
+
+            def step(cc, carry):
+                tile_of(to, cc, list(range(32)))
+                return carry
+
+            lax.fori_loop(0, tiles, step, 0)
+        else:
+
+            def step(n, carry):
+                if p == 1:
+                    decoders = [y * 8 + to * 2 + c for y in range(4) for c in range(2)]
+                else:
+                    decoders = [to * 8 + x * 2 + c for x in range(4) for c in range(2)]
+                tile_of(n // tiles, n % tiles, decoders)
+                return carry
+
+            lax.fori_loop(0, 4 * tiles, step, 0)
 
     def reach(p, stage, to):
         first, second, third = ORDERS[p]
@@ -583,33 +605,56 @@
             return core * 64 + at[third] * 16 + to * 4, 4
         return core * 64 + at[third] * 16 + at[second] * 4 + to, 1
 
+    def set_of(p, n):
+        return (at[ORDERS[p][2]] + n + 1) % 4
+
+    def swap_copy(p, n):
+        to = set_of(p, n)
+        return remote(
+            cs[p].at[pl.ds((1 - core) * 64 + to * 16, 16)],
+            rcs[p].at[pl.ds(to * 16, 16)],
+            RS + p * 13 + n,
+            sibling,
+        )
+
+    def scatter_copy(p, stage, step):
+        axis = ORDERS[p][2 - stage]
+        begin, count = reach(p, stage, (at[axis] + step) % 4)
+        return remote(
+            cs[p].at[pl.ds(begin, count)],
+            rstage[stage][p].at[pl.ds((step - 1) * count, count)],
+            RS + p * 13 + 4 + stage * 3 + step - 1,
+            peer(axis, step),
+        )
+
     def scatter_start(p, stage):
-        axis = ORDERS[p][2 - stage]
         for step in (1, 2, 3):
-            begin, count = reach(p, stage, (at[axis] + step) % 4)
-            start(
-                cs[p].at[pl.ds(begin, count)],
-                rstage[stage][p].at[pl.ds((step - 1) * count, count)],
-                RS + p * 10 + 1 + stage * 3 + step - 1,
-                peer(axis, step),
-            )
-
-    def swap_finish(p):
-        arrived(rcs[p], RS + p * 10)
+            copy = scatter_copy(p, stage, step)
+            copy.start()
+            started.append(copy)
+
+    def swap_finish(p, n):
+        to = set_of(p, n)
+        arrived(rcs[p].at[pl.ds(to * 16, 16)], RS + p * 13 + n)
 
         def step(b, carry):
-            _, block = add_blocks(p, [cs[p][core * 64 + b], rcs[p][b]])
-            cs[p][core * 64 + b] = block
+            mine_at = core * 64 + to * 16 + b
+            _, block = add_blocks(p, [cs[p][mine_at], rcs[p][to * 16 + b]])
+            cs[p][mine_at] = block
             return carry
 
-        lax.fori_loop(0, 64, step, 0)
+        lax.fori_loop(0, 16, step, 0)
+
+        @pl.when(n < 3)
+        def _():
+            scatter_copy(p, 0, n + 1).start()
 
     def scatter_wait(p, stage):
         count = (16, 4, 1)[stage]
         for step in (1, 2, 3):
             arrived(
                 rstage[stage][p].at[pl.ds((step - 1) * count, count)],
-                RS + p * 10 + 1 + stage * 3 + step - 1,
+                RS + p * 13 + 4 + stage * 3 + step - 1,
             )
 
     def scatter_add(p, stage):
@@ -625,18 +670,25 @@
 
         lax.fori_loop(0, count, step, 0)
 
-    context_of(0, 3)
-    swap_start(0)
-    context_of(1, 3)
-    swap_start(1)
-    swap_finish(0)
-    scatter_start(0, 0)
-    context_of(2, 2)
-    swap_start(2)
-    swap_finish(1)
-    scatter_start(1, 0)
-    swap_finish(2)
-    scatter_start(2, 0)
+    def scatter_set(n, carry):
+        for p in range(3):
+            context_set(p, set_of(p, n))
+            swap_copy(p, n).start()
+            if p > 0:
+                swap_finish(p - 1, n)
+            else:
+
+                @pl.when(n > 0)
+                def _():
+                    swap_finish(2, n - 1)
+
+        return carry
+
+    lax.fori_loop(0, 4, scatter_set, 0)
+    swap_finish(2, 3)
+    for p in range(3):
+        started.extend(swap_copy(p, n) for n in range(4))
+        started.extend(scatter_copy(p, 0, step) for step in (1, 2, 3))
 
     coefficient = (LOSS_WEIGHT * E ** (-0.5)) * (jnp.exp(log_prob) - target)
     grads = jnp.where(valid, coefficient * emb, 0.0).astype(BF16)
@@ -711,10 +763,12 @@
         pltpu.VMEM((4, 32, 128), jnp.int32),
         pltpu.VMEM((8, 128), jnp.int32),
         pltpu.VMEM((8, 128), jnp.int32),
+        pltpu.VMEM((16, 128), jnp.int32),
+        pltpu.SMEM((16, 128), jnp.int32),
         pltpu.VMEM((128, 128), F32),
         pltpu.SemaphoreType.DMA((SEMS,)),
         pltpu.SemaphoreType.DMA((SEMS,)),
-        pltpu.SemaphoreType.DMA((9,)),
+        pltpu.SemaphoreType.DMA((10,)),
     ]
     context, loss, grad = pl.pallas_call(
         kernel,

time: 101 us -> 95.6 us (0.947)
  Pallas kernels: 100 us -> 94.8 us
    pallas_call x1, Pallas kernels: 98.7 us -> 93.1 us  [body(): pl.pallas_call(kernel, out_shape=(jax.ShapeDtypeStruct((1, 8, D), BF16),...]
where the time goes in v3:
time: 95.6 us; the launch traced here: 95.4 us
  Pallas kernels  94.8 us (99%)
    pallas_call x1, Pallas kernels, body(): pl.pallas_call(kernel, out_shape=(jax.ShapeDtypeStruct((1, 8, D), BF16),...  93.1 us

profile of v3, /device:TPU:0, one launch (start us, length us, event | category | flops | bytes accessed | tf_op | source)
XLA Modules:
  0.0 95.4 jit_solution(4735557643112368280)
XLA Ops:
  0.6 93.1 %shard_map.121 = (bf16[1,8,2048]{2,1,0:T(8,128)(2,1)}, f32[8,128]{1,0:T(8,128)}, f32[64,768]{1,0:T(8,128)}) custom-call(s32[32,128]{1,0:T(8,128)} %bitcast.4, s32[64,128]{1,0:T(8,128)} %bitcast.3, s32[1,32]{1,0:T(1,128)} %rq_ref.1, bf16[64,8,2048]{2,1,0:T(8,128)(2,1)} %states_ref.1, bf16[64,768]{1,0:T(8,128)(2,1)} %keys_ref.1, ...), custom_call_target="tpu_custom_call" | custom-call | flops 12000000000 | bytes 20000000 | tf_op jit(solution)/shard_map/pallas_call | solution.py:773
  93.8 1.7 %shard_map.122 = (bf16[1,8,2048]{2,1,0:T(8,128)(2,1)}, f32[1]{0:T(128)}, f32[64,768]{1,0:T(8,128)}) custom-call(bf16[1,8,2048]{2,1,0:T(8,128)(2,1)} %get-tuple-element.6.ctx_ref, f32[8,128]{1,0:T(8,128)} %get-tuple-element.7.loss_ref, f32[64,768]{1,0:T(8,128)} %get-tuple-element.8.grad_ref), custom_call_target="tpu_custom_call" | custom-call | tf_op jit(solution)/shard_map/pallas_call | solution.py:812

commit v4 on v3

--- a/solution.py
+++ b/solution.py
@@ -81,6 +81,7 @@
     pick,
     nrm,
     kv,
+    keys_t,
     q0,
     q1,
     q2,
@@ -296,6 +297,25 @@
     k_row = (code_row64 // 128) % 32
     row_row = code_row64 % 128 - 1
 
+    for p in range(3):
+        for step in (1, 2, 3):
+            gather_wait(p, 1, step)
+    gather_start(2)
+    for p in range(3):
+        forward(p, 0)
+
+    for step in (1, 2, 3):
+        arrived(rqt.at[(my_group + 4 - step) % 4], RQ + step - 1)
+    for g in range(4):
+        match = rqt[g] == lane_ref[g : g + 1, :]
+        row = jnp.sum(jnp.where(match, iota((32, 128), 0) + (g * 32 + 1), 0), axis=0, keepdims=True)
+        ir_ref[g : g + 1, :] = row - 1
+    decoder_of = jnp.maximum(ir_ref[0:4, :], 0)
+    for p in range(3):
+        block_ref[p * 4 : p * 4 + 4, :] = block_of(p, decoder_of // 32, decoder_of % 32)
+    block_copy = pltpu.make_async_copy(block_ref, block_smem, local_sem.at[9])
+    block_copy.start()
+
     states_copy.wait()
 
     def norm_pair(pair, carry):
@@ -310,25 +330,6 @@
 
     lax.fori_loop(0, 32, norm_pair, 0)
 
-    for p in range(3):
-        for step in (1, 2, 3):
-            gather_wait(p, 1, step)
-    gather_start(2)
-    for p in range(3):
-        forward(p, 0)
-
-    for step in (1, 2, 3):
-        arrived(rqt.at[(my_group + 4 - step) % 4], RQ + step - 1)
-    for g in range(4):
-        match = rqt[g] == lane_ref[g : g + 1, :]
-        row = jnp.sum(jnp.where(match, iota((32, 128), 0) + (g * 32 + 1), 0), axis=0, keepdims=True)
-        ir_ref[g : g + 1, :] = row - 1
-    decoder_of = jnp.maximum(ir_ref[0:4, :], 0)
-    for p in range(3):
-        block_ref[p * 4 : p * 4 + 4, :] = block_of(p, decoder_of // 32, decoder_of % 32)
-    block_copy = pltpu.make_async_copy(block_ref, block_smem, local_sem.at[9])
-    block_copy.start()
-
     def pick_step(n, carry):
         cols = pl.ds(pl.multiple_of(n * 256, 256), 256)
         nrm[:, cols] = nn(pick[...], stored[:, cols]).astype(BF16)
@@ -346,12 +347,18 @@
             w_copies[n].wait()
         lax.fori_loop(begin * 2, end * 2, step, 0)
 
-    project(0, 6)
+    project(0, 4)
     for step in (1, 3, 2):
         for p in range(3):
             gather_wait(p, 2, step)
             forward(p, step)
-    project(6, 8)
+    def turn(n, carry):
+        rows = pl.ds(pl.multiple_of(n * 256, 256), 256)
+        keys_t[rows, :] = jnp.transpose(kv[:, rows].astype(F32)).astype(BF16)
+        return carry
+
+    lax.fori_loop(0, 8, turn, 0)
+    project(4, 6)
     block_copy.wait()
 
     for p in range(3):
@@ -364,32 +371,33 @@
     high = (lane >= 64).astype(F32).astype(BF16)
 
     def scores_of(p, tiles):
-        def step(n, carry):
-            g, cc = n // tiles, n % tiles
+        def step(cc, carry):
             inner = pl.multiple_of(cc * 128, 128)
             outer = pl.multiple_of((3 * p + cc) * 128, 128)
-            slots = pl.ds(pl.multiple_of(g * 128, 128), 128)
-            right = jnp.concatenate(
-                [kv[slots, pl.ds(outer, 128)], kv[slots, pl.ds(outer + 1024, 128)]], axis=0
-            )
-            left = []
-            for r in range(SLOTS):
-                block = qs[p][block_smem[p * 4 + g, r * 8], :, pl.ds(inner, 128)]
-                left += [block * low, block * high]
-            out = nt(jnp.concatenate(left, axis=0), right)
-            total = [jnp.zeros((8, 128), F32) for _ in range(4)]
-            for r in range(SLOTS):
-                keep = jnp.broadcast_to(lane // 8 == r, (8, 128))
-                for tile in range(4):
-                    half = tile % 2
-                    begin = r * 32 + tile * 8
-                    piece = out[begin : begin + 8, half * 128 : half * 128 + 128]
-                    total[tile] = jnp.where(keep, piece, total[tile])
             rows = pl.ds(pl.multiple_of((3 * p + cc) * 32, 32), 32)
-            s_buf[g, rows, :] = jnp.concatenate(total, axis=0) * (64 ** (-0.5))
+            for g in range(4):
+                slots = slice(g * 128, g * 128 + 128)
+                right = jnp.concatenate(
+                    [keys_t[pl.ds(outer, 128), slots], keys_t[pl.ds(outer + 1024, 128), slots]],
+                    axis=1,
+                )
+                left = []
+                for r in range(SLOTS):
+                    block = qs[p][block_smem[p * 4 + g, r * 8], :, pl.ds(inner, 128)]
+                    left += [block * low, block * high]
+                out = nn(jnp.concatenate(left, axis=0), right)
+                total = [jnp.zeros((8, 128), F32) for _ in range(4)]
+                for r in range(SLOTS):
+                    keep = jnp.broadcast_to(lane // 8 == r, (8, 128))
+                    for tile in range(4):
+                        half = tile % 2
+                        begin = r * 32 + tile * 8
+                        piece = out[begin : begin + 8, half * 128 : half * 128 + 128]
+                        total[tile] = jnp.where(keep, piece, total[tile])
+                s_buf[g, rows, :] = jnp.concatenate(total, axis=0) * (64 ** (-0.5))
             return carry
 
-        lax.fori_loop(0, 4 * tiles, step, 0)
+        lax.fori_loop(0, tiles, step, 0)
 
     scores_of(0, 3)
     scores_of(1, 3)
@@ -431,6 +439,14 @@
     )
     t0[...] = table[0:128, :]
     t1[...] = table[128:256, :]
+    size = (64, 64, 16)
+
+    def table_swap(p):
+        other = pl.ds(pl.multiple_of((1 - core) * size[p], size[p]), size[p])
+        start(ts[p].at[other], acs[p], AR + p * 11, sibling)
+
+    table_swap(0)
+    table_swap(1)
 
     lane64 = iota((64, 128), 1)
     i_cols = []
@@ -453,8 +469,8 @@
     retrieval_row = jnp.sum(jnp.where(square, retrieval, 0.0), axis=0, keepdims=True)
     by_k = jnp.where(iota((32, 64), 0) == k_row, retrieval_row, 0.0)
     t2[...] = nn(by_k, hot_i, HIGHEST)
-
-    size = (64, 64, 16)
+    table_swap(2)
+
 
     def combine(p, values):
         if p == 2:
@@ -471,9 +487,6 @@
         return top + jnp.log(total)
 
     for p in range(3):
-        other = pl.ds(pl.multiple_of((1 - core) * size[p], size[p]), size[p])
-        start(ts[p].at[other], acs[p], AR + p * 11, sibling)
-    for p in range(3):
         own = pl.ds(pl.multiple_of(core * size[p], size[p]), size[p])
         arrived(acs[p], AR + p * 11)
         accs[p][0] = combine(p, [ts[p][own, :], acs[p][...]])
@@ -485,6 +498,8 @@
                 peer(ORDERS[p][0], step),
             )
     for stage in range(3):
+        if stage < 2:
+            project(6 + stage, 7 + stage)
         for p in range(3):
             values = [accs[p][stage]]
             for step in (1, 2, 3):
@@ -531,15 +546,18 @@
     loss_col = jnp.sum(jnp.where(sub == lanes, loss_row, 0.0), axis=1, keepdims=True)
     loss_t[...] = jnp.broadcast_to(loss_col, (128, 128))
 
-    def loss_block(j, carry):
-        for g in range(4):
-            value = jnp.broadcast_to(loss_t[pl.ds(g * 32 + j, 1), :], (8, 128))
-            top_half = value.astype(BF16).astype(F32)
-            tile = jnp.concatenate([top_half, value - top_half], axis=0)
-            c2[block_of(2, g, j), :, 256:384] = tile.astype(BF16)
-        return carry
-
-    lax.fori_loop(0, 32, loss_block, 0)
+    def loss_set(to):
+        def step(g, carry):
+            for x in range(4):
+                for c in range(2):
+                    j = to * 8 + x * 2 + c
+                    value = jnp.broadcast_to(loss_t[pl.ds(g * 32 + j, 1), :], (8, 128))
+                    top_half = value.astype(BF16).astype(F32)
+                    tile = jnp.concatenate([top_half, value - top_half], axis=0)
+                    c2[block_of(2, g, j), :, 256:384] = tile.astype(BF16)
+            return carry
+
+        lax.fori_loop(0, 4, step, 0)
 
     keep_low = jnp.broadcast_to(lane < 64, (8, 128))
 
@@ -547,14 +565,14 @@
         tiles = 2 if p == 2 else 3
 
         def tile_of(g, cc, decoders):
-            inner = pl.multiple_of(cc * 128, 128)
-            outer = pl.multiple_of(D + (3 * p + cc) * 128, 128)
+            inner = cc * 128
+            outer = D + (3 * p + cc) * 128
             slots = pl.ds(pl.multiple_of(g * 128, 128), 128)
             right = jnp.concatenate(
                 [kv[slots, pl.ds(outer, 128)], kv[slots, pl.ds(outer + 1024, 128)]], axis=1
             )
             row = ir_ref[pl.ds(g, 1), :] - g * 32
-            rows = pl.ds(pl.multiple_of((3 * p + cc) * 32, 32), 32)
+            rows = pl.ds((3 * p + cc) * 32, 32)
             weights = p_buf[g, rows, :]
             for first in range(0, len(decoders), 16):
                 batch = decoders[first : first + 16]
@@ -580,22 +598,24 @@
 
         if p == 0:
 
-            def step(cc, carry):
+            for cc in range(tiles):
                 tile_of(to, cc, list(range(32)))
-                return carry
-
-            lax.fori_loop(0, tiles, step, 0)
         else:
+
+            if p == 2:
+                loss_set(to)
 
             def step(n, carry):
                 if p == 1:
                     decoders = [y * 8 + to * 2 + c for y in range(4) for c in range(2)]
                 else:
                     decoders = [to * 8 + x * 2 + c for x in range(4) for c in range(2)]
-                tile_of(n // tiles, n % tiles, decoders)
+                for g in (2 * n, 2 * n + 1):
+                    for cc in range(tiles):
+                        tile_of(g, cc, decoders)
                 return carry
 
-            lax.fori_loop(0, 4 * tiles, step, 0)
+            lax.fori_loop(0, 2, step, 0)
 
     def reach(p, stage, to):
         first, second, third = ORDERS[p]
@@ -637,13 +657,17 @@
         to = set_of(p, n)
         arrived(rcs[p].at[pl.ds(to * 16, 16)], RS + p * 13 + n)
 
-        def step(b, carry):
-            mine_at = core * 64 + to * 16 + b
-            _, block = add_blocks(p, [cs[p][mine_at], rcs[p][to * 16 + b]])
-            cs[p][mine_at] = block
+        def step(four, carry):
+            places = [four * 4 + n for n in range(4)]
+            sums = [
+                add_blocks(p, [cs[p][core * 64 + to * 16 + b], rcs[p][to * 16 + b]])[1]
+                for b in places
+            ]
+            for b, block in zip(places, sums):
+                cs[p][core * 64 + to * 16 + b] = block
             return carry
 
-        lax.fori_loop(0, 16, step, 0)
+        lax.fori_loop(0, 4, step, 0)
 
         @pl.when(n < 3)
         def _():
@@ -662,13 +686,17 @@
         begin, count = reach(p, stage, at[axis])
         scatter_wait(p, stage)
 
-        def step(b, carry):
-            parts = [rstage[stage][p][n * count + b] for n in range(3)]
-            _, block = add_blocks(p, [cs[p][begin + b]] + parts)
-            cs[p][begin + b] = block
+        def step(four, carry):
+            sums = []
+            for n in range(4):
+                b = four * 4 + n
+                parts = [rstage[stage][p][n * count + b] for n in range(3)]
+                sums.append((b, add_blocks(p, [cs[p][begin + b]] + parts)[1]))
+            for b, block in sums:
+                cs[p][begin + b] = block
             return carry
 
-        lax.fori_loop(0, count, step, 0)
+        lax.fori_loop(0, count // 4, step, 0)
 
     def scatter_set(n, carry):
         for p in range(3):
@@ -746,6 +774,7 @@
         pltpu.VMEM((512, 512), BF16),
         pltpu.VMEM((512, D), BF16),
         pltpu.VMEM((512, 2 * D), BF16),
+        pltpu.VMEM((D, 512), BF16),
     ]
     scratch += [pltpu.VMEM((128, 16, 384), BF16)] * 6
     scratch += [pltpu.VMEM((64, 16, 384), BF16)] * 3

time: 95.6 us -> 85.8 us (0.90)
  Pallas kernels: 94.8 us -> 84.4 us
    pallas_call x1, Pallas kernels: 93.1 us -> 82.7 us  [body(): pl.pallas_call(kernel, out_shape=(jax.ShapeDtypeStruct((1, 8, D), BF16),...]
where the time goes in v4:
time: 85.8 us; the launch traced here: 85 us
  Pallas kernels  84.4 us (98%)
    pallas_call x1, Pallas kernels, body(): pl.pallas_call(kernel, out_shape=(jax.ShapeDtypeStruct((1, 8, D), BF16),...  82.7 us

profile of v4, /device:TPU:0, one launch (start us, length us, event | category | flops | bytes accessed | tf_op | source)
XLA Modules:
  0.0 85.0 jit_solution(15511331522386650480)
XLA Ops:
  0.6 82.7 %shard_map.121 = (bf16[1,8,2048]{2,1,0:T(8,128)(2,1)}, f32[8,128]{1,0:T(8,128)}, f32[64,768]{1,0:T(8,128)}) custom-call(s32[32,128]{1,0:T(8,128)} %bitcast.4, s32[64,128]{1,0:T(8,128)} %bitcast.3, s32[1,32]{1,0:T(1,128)} %rq_ref.1, bf16[64,8,2048]{2,1,0:T(8,128)(2,1)} %states_ref.1, bf16[64,768]{1,0:T(8,128)(2,1)} %keys_ref.1, ...), custom_call_target="tpu_custom_call" | custom-call | flops 12000000000 | bytes 20000000 | tf_op jit(solution)/shard_map/pallas_call | solution.py:802
  83.4 1.7 %shard_map.122 = (bf16[1,8,2048]{2,1,0:T(8,128)(2,1)}, f32[1]{0:T(128)}, f32[64,768]{1,0:T(8,128)}) custom-call(bf16[1,8,2048]{2,1,0:T(8,128)(2,1)} %get-tuple-element.6.ctx_ref, f32[8,128]{1,0:T(8,128)} %get-tuple-element.7.loss_ref, f32[64,768]{1,0:T(8,128)} %get-tuple-element.8.grad_ref), custom_call_target="tpu_custom_call" | custom-call | tf_op jit(solution)/shard_map/pallas_call | solution.py:841

commit v5 on v4

--- a/solution.py
+++ b/solution.py
@@ -24,8 +24,8 @@
 ABSENT = -1e30
 
 ORDERS = (("x", "y", "z"), ("y", "z", "x"), ("z", "x", "y"))
-AG, AG_SIB, RQ, AR, RS = 0, 27, 39, 42, 75
-SEMS = 114
+AG, AG_SIB, RQ, SWAP, AR, FIN, RS, LOSS = 0, 27, 39, 42, 44, 71, 74, 113
+SEMS = 126
 
 
 def nt(a, b, precision=None):
@@ -49,16 +49,14 @@
     return core * 64 + at[third] * 16 + at[second] * 4 + at[first]
 
 
-def add_blocks(part, blocks):
-    total = blocks[0].astype(F32)
-    for block in blocks[1:]:
-        total = total + block.astype(F32)
-    if part < 2:
-        return total, total.astype(BF16)
-    loss = total[0:8, 256:384] + total[8:16, 256:384]
-    high = loss.astype(BF16).astype(F32)
-    tile = jnp.concatenate([high, loss - high], axis=0)
-    return total, jnp.concatenate([total[:, 0:256], tile], axis=1).astype(BF16)
+def log_add(values):
+    top = values[0]
+    for value in values[1:]:
+        top = jnp.maximum(top, value)
+    total = jnp.exp(values[0] - top)
+    for value in values[1:]:
+        total = total + jnp.exp(value - top)
+    return top + jnp.log(total)
 
 
 def kernel(
@@ -102,40 +100,25 @@
     rd2,
     s_buf,
     p_buf,
-    t0,
-    t1,
-    t2,
-    ac0,
-    ac1,
-    ac2,
-    ar0,
-    ar1,
-    ar2,
-    acc0,
-    acc1,
-    acc2,
-    l0,
-    l1,
-    l2,
+    t_ref,
+    o_ref,
+    accs,
+    ars,
+    fin,
+    e_ref,
+    e_in,
     rqt,
     lane_ref,
     ir_ref,
+    lam_ref,
     block_ref,
     block_smem,
-    loss_t,
     send_sem,
     recv_sem,
     local_sem,
 ):
     qs, cs, rcs = (q0, q1, q2), (c0, c1, c2), (rc0, rc1, rc2)
     rstage = ((ra0, ra1, ra2), (rb0, rb1, rb2), (rd0, rd1, rd2))
-    ts, acs, ars, accs, ls = (
-        (t0, t1, t2),
-        (ac0, ac1, ac2),
-        (ar0, ar1, ar2),
-        (acc0, acc1, acc2),
-        (l0, l1, l2),
-    )
     my_group = lax.axis_index("group")
     my_dev = lax.axis_index("dev")
     core = my_dev % 2
@@ -170,6 +153,16 @@
 
     def arrived(dst, number):
         remote(dst, dst, number, sibling).wait_recv()
+
+    def cross(step):
+        return (my_group, at["y"] * 8 + (at["x"] + step) % 4 * 2 + 1 - core)
+
+    barrier = pltpu.get_barrier_semaphore()
+    pl.semaphore_signal(barrier, inc=1, device_id=sibling, device_id_type=MESH)
+    for step in (1, 2, 3):
+        for axis in ("x", "y", "z"):
+            pl.semaphore_signal(barrier, inc=1, device_id=peer(axis, step), device_id_type=MESH)
+        pl.semaphore_signal(barrier, inc=1, device_id=cross(step), device_id_type=MESH)
 
     states_copy = pltpu.make_async_copy(states_ref, st, local_sem.at[8])
     states_copy.start()
@@ -204,12 +197,7 @@
     rq_col = jnp.sum(jnp.where(diagonal, rq_ref[...], 0), axis=1, keepdims=True)
     rqt[my_group] = jnp.broadcast_to(rq_col, (32, 128))
 
-    barrier = pltpu.get_barrier_semaphore()
-    pl.semaphore_signal(barrier, inc=1, device_id=sibling, device_id_type=MESH)
-    for axis in ("x", "y", "z"):
-        for step in (1, 2, 3):
-            pl.semaphore_signal(barrier, inc=1, device_id=peer(axis, step), device_id_type=MESH)
-    pl.semaphore_wait(barrier, 10)
+    pl.semaphore_wait(barrier, 13)
 
     def span(p, stage, back):
         first, second, third = ORDERS[p]
@@ -313,6 +301,7 @@
     decoder_of = jnp.maximum(ir_ref[0:4, :], 0)
     for p in range(3):
         block_ref[p * 4 : p * 4 + 4, :] = block_of(p, decoder_of // 32, decoder_of % 32)
+    lam_ref[0:4, :] = jnp.where(ir_ref[0:4, :] >= 0, block_ref[0:4, :], -1)
     block_copy = pltpu.make_async_copy(block_ref, block_smem, local_sem.at[9])
     block_copy.start()
 
@@ -358,7 +347,7 @@
         return carry
 
     lax.fori_loop(0, 8, turn, 0)
-    project(4, 6)
+    project(4, 7)
     block_copy.wait()
 
     for p in range(3):
@@ -374,7 +363,8 @@
         def step(cc, carry):
             inner = pl.multiple_of(cc * 128, 128)
             outer = pl.multiple_of((3 * p + cc) * 128, 128)
-            rows = pl.ds(pl.multiple_of((3 * p + cc) * 32, 32), 32)
+            rows = pl.ds(pl.multiple_of((3 * p + cc) * 16, 16), 16)
+            high_rows = pl.ds(pl.multiple_of((3 * p + cc) * 16 + 128, 16), 16)
             for g in range(4):
                 slots = slice(g * 128, g * 128 + 128)
                 right = jnp.concatenate(
@@ -394,7 +384,8 @@
                         begin = r * 32 + tile * 8
                         piece = out[begin : begin + 8, half * 128 : half * 128 + 128]
                         total[tile] = jnp.where(keep, piece, total[tile])
-                s_buf[g, rows, :] = jnp.concatenate(total, axis=0) * (64 ** (-0.5))
+                s_buf[g, rows, :] = jnp.concatenate(total[0:2], axis=0) * (64 ** (-0.5))
+                s_buf[g, high_rows, :] = jnp.concatenate(total[2:4], axis=0) * (64 ** (-0.5))
             return carry
 
         lax.fori_loop(0, tiles, step, 0)
@@ -426,7 +417,7 @@
                 jnp.broadcast_to(same, (256, 128)), pltpu.roll(peak, 128 - s, 1), ABSENT
             )
             peak = jnp.maximum(peak, other)
-        chosen = sub == ir_ref[g : g + 1, :]
+        chosen = sub == lam_ref[g : g + 1, :]
         first = ((before != u_row) | (lane < 8)) & (lane % 8 == 0)
         lead = jnp.where(chosen & jnp.broadcast_to(first, (128, 128)), 1.0, 0.0)
         peak_i = peak_i + nt(peak, lead, HIGHEST)
@@ -437,24 +428,18 @@
         peak_i + jnp.log(jnp.maximum(total_i, 1e-30)),
         ABSENT,
     )
-    t0[...] = table[0:128, :]
-    t1[...] = table[128:256, :]
-    size = (64, 64, 16)
-
-    def table_swap(p):
-        other = pl.ds(pl.multiple_of((1 - core) * size[p], size[p]), size[p])
-        start(ts[p].at[other], acs[p], AR + p * 11, sibling)
-
-    table_swap(0)
-    table_swap(1)
+    t_ref[0:256, :] = table
+    start(t_ref.at[pl.ds(0, 256)], o_ref.at[pl.ds(0, 256)], SWAP, sibling)
 
     lane64 = iota((64, 128), 1)
-    i_cols = []
+    i_cols, lam_cols = [], []
     for g in range(4):
         picked = jnp.where(slot16, ir_ref[g : g + 1, :] + 1, 0)
         i_cols.append(jnp.sum(picked, axis=1, keepdims=True))
+        picked = jnp.where(slot16, lam_ref[g : g + 1, :] + 1, 0)
+        lam_cols.append(jnp.sum(picked, axis=1, keepdims=True))
     i_col = jnp.concatenate(i_cols, axis=0) - 1
-    one_hot_i = lane64 == i_col
+    one_hot_i = lane64 == jnp.concatenate(lam_cols, axis=0) - 1
     hot_i = jnp.where(one_hot_i, 1.0, 0.0)
     decoder = jnp.maximum(i_col, 0)
     place = block_of(2, decoder // 32, decoder % 32) * 16
@@ -468,96 +453,59 @@
     retrieval = jnp.sum(emb * keys, axis=1, keepdims=True) * (E ** (-0.5))
     retrieval_row = jnp.sum(jnp.where(square, retrieval, 0.0), axis=0, keepdims=True)
     by_k = jnp.where(iota((32, 64), 0) == k_row, retrieval_row, 0.0)
-    t2[...] = nn(by_k, hot_i, HIGHEST)
-    table_swap(2)
-
-
-    def combine(p, values):
-        if p == 2:
-            total = values[0]
-            for value in values[1:]:
-                total = total + value
-            return total
-        top = values[0]
-        for value in values[1:]:
-            top = jnp.maximum(top, value)
-        total = jnp.exp(values[0] - top)
-        for value in values[1:]:
-            total = total + jnp.exp(value - top)
-        return top + jnp.log(total)
-
-    for p in range(3):
-        own = pl.ds(pl.multiple_of(core * size[p], size[p]), size[p])
-        arrived(acs[p], AR + p * 11)
-        accs[p][0] = combine(p, [ts[p][own, :], acs[p][...]])
-        for step in (1, 2, 3):
-            start(
-                accs[p].at[0],
-                ars[p].at[step - 1],
-                AR + p * 11 + step,
-                peer(ORDERS[p][0], step),
-            )
-    for stage in range(3):
-        if stage < 2:
-            project(6 + stage, 7 + stage)
+    t_ref[256:288, :] = nn(by_k, hot_i, HIGHEST)
+    start(t_ref.at[pl.ds(256, 32)], o_ref.at[pl.ds(256, 32)], SWAP + 1, sibling)
+    project(7, 8)
+
+    low_lanes = lane < 64
+
+    def pack(first, second, of):
+        zero = jnp.where(low_lanes, first, pltpu.roll(second, 64, 1))
+        one = jnp.where(low_lanes, pltpu.roll(first, 64, 1), second)
+        return jnp.where(of == 0, zero, one)
+
+    arrived(o_ref.at[pl.ds(0, 256)], SWAP)
+    arrived(o_ref.at[pl.ds(256, 32)], SWAP + 1)
+    pair = log_add([t_ref[0:256, :], o_ref[0:256, :]])
+    pair_raw = t_ref[256:288, :] + o_ref[256:288, :]
+    packed = pack(pair[0:128], pair[128:256], core)
+    accs[0, 0] = packed[0:48]
+    accs[1, 0] = packed[48:96]
+    accs[2, 0] = jnp.concatenate([packed[96:128], pack(pair_raw[0:16], pair_raw[16:32], core)], axis=0)
+
+    def table_copy(p, stage, step):
+        return remote(
+            accs.at[p, stage],
+            ars.at[p, stage * 3 + step - 1],
+            AR + p * 9 + stage * 3 + step - 1,
+            peer(ORDERS[p][2 - stage], step),
+        )
+
+    def table_start(stage):
         for p in range(3):
-            values = [accs[p][stage]]
             for step in (1, 2, 3):
-                arrived(ars[p].at[stage * 3 + step - 1], AR + p * 11 + stage * 3 + step)
-                values.append(ars[p][stage * 3 + step - 1])
-            total = combine(p, values)
-            own = pl.ds(pl.multiple_of(core * size[p], size[p]), size[p])
-            if stage == 2:
-                ls[p][own, :] = total
-                ref = ls[p].at[own]
-                start(ref, ref, AR + p * 11 + 10, sibling)
+                table_copy(p, stage, step).start()
+
+    def table_finish(stage):
+        for p in range(3):
+            values = [accs[p, stage]]
+            for step in (1, 2, 3):
+                arrived(ars.at[p, stage * 3 + step - 1], AR + p * 9 + stage * 3 + step - 1)
+                values.append(ars[p, stage * 3 + step - 1])
+            if p < 2:
+                accs[p, stage + 1] = log_add(values)
             else:
-                accs[p][stage + 1] = total
-                for step in (1, 2, 3):
-                    start(
-                        accs[p].at[stage + 1],
-                        ars[p].at[(stage + 1) * 3 + step - 1],
-                        AR + p * 11 + (stage + 1) * 3 + step,
-                        peer(ORDERS[p][stage + 1], step),
-                    )
-    for p in range(3):
-        other = pl.ds(pl.multiple_of((1 - core) * size[p], size[p]), size[p])
-        arrived(ls[p].at[other], AR + p * 11 + 10)
-
-    log_sum = jnp.concatenate([l0[...], l1[...]], axis=0)
-    targets = []
+                raw = values[0][32:48] + values[1][32:48] + values[2][32:48] + values[3][32:48]
+                total = log_add([value[0:32] for value in values])
+                accs[p, stage + 1] = jnp.concatenate([total, raw], axis=0)
+
+    table_start(0)
+    while started:
+        started.pop(0).wait_send()
+
     for g in range(4):
-        chosen = jnp.where(sub == ir_ref[g : g + 1, :], 1.0, 0.0)
-        weights = jnp.exp(s_buf[g] - nn(log_sum, chosen, HIGHEST))
-        p_buf[g] = weights.astype(BF16)
-        mass = jnp.sum(weights, axis=0, keepdims=True)
-        own = iota((16, 128), 1) // 8 == iota((16, 128), 0)
-        targets.append(jnp.sum(jnp.where(own, mass, 0.0), axis=1, keepdims=True))
-    target = jnp.concatenate(targets, axis=0) * (1.0 / 256.0)
-    raw = l2[...]
-    top = jnp.max(raw, axis=0, keepdims=True)
-    log_prob_all = raw - top - jnp.log(jnp.sum(jnp.exp(raw - top), axis=0, keepdims=True))
-    hot_k = jnp.where(iota((64, 32), 1) == k_col, 1.0, 0.0)
-    log_prob = jnp.sum(
-        jnp.where(one_hot_i, nn(hot_k, log_prob_all, HIGHEST), 0.0), axis=1, keepdims=True
-    )
-    term = jnp.where(valid, target * (jnp.log(target) - log_prob), 0.0)
-    loss_row = jnp.sum(jnp.where(one_hot_i, term, 0.0), axis=0, keepdims=True)
-    loss_col = jnp.sum(jnp.where(sub == lanes, loss_row, 0.0), axis=1, keepdims=True)
-    loss_t[...] = jnp.broadcast_to(loss_col, (128, 128))
-
-    def loss_set(to):
-        def step(g, carry):
-            for x in range(4):
-                for c in range(2):
-                    j = to * 8 + x * 2 + c
-                    value = jnp.broadcast_to(loss_t[pl.ds(g * 32 + j, 1), :], (8, 128))
-                    top_half = value.astype(BF16).astype(F32)
-                    tile = jnp.concatenate([top_half, value - top_half], axis=0)
-                    c2[block_of(2, g, j), :, 256:384] = tile.astype(BF16)
-            return carry
-
-        lax.fori_loop(0, 4, step, 0)
+        chosen = jnp.where(sub == lam_ref[g : g + 1, :], 1.0, 0.0)
+        p_buf[g] = jnp.exp(s_buf[g] - nn(pair, chosen, HIGHEST)).astype(BF16)
 
     keep_low = jnp.broadcast_to(lane < 64, (8, 128))
 
@@ -572,8 +520,10 @@
                 [kv[slots, pl.ds(outer, 128)], kv[slots, pl.ds(outer + 1024, 128)]], axis=1
             )
             row = ir_ref[pl.ds(g, 1), :] - g * 32
-            rows = pl.ds((3 * p + cc) * 32, 32)
-            weights = p_buf[g, rows, :]
+            c = 3 * p + cc
+            weights = jnp.concatenate(
+                [p_buf[g, pl.ds(c * 16, 16), :], p_buf[g, pl.ds(128 + c * 16, 16), :]], axis=0
+            )
             for first in range(0, len(decoders), 16):
                 batch = decoders[first : first + 16]
                 left = []
@@ -602,9 +552,6 @@
                 tile_of(to, cc, list(range(32)))
         else:
 
-            if p == 2:
-                loss_set(to)
-
             def step(n, carry):
                 if p == 1:
                     decoders = [y * 8 + to * 2 + c for y in range(4) for c in range(2)]
@@ -660,7 +607,9 @@
         def step(four, carry):
             places = [four * 4 + n for n in range(4)]
             sums = [
-                add_blocks(p, [cs[p][core * 64 + to * 16 + b], rcs[p][to * 16 + b]])[1]
+                (
+                    cs[p][core * 64 + to * 16 + b].astype(F32) + rcs[p][to * 16 + b].astype(F32)
+                ).astype(BF16)
                 for b in places
             ]
             for b, block in zip(places, sums):
@@ -681,22 +630,45 @@
                 RS + p * 13 + 4 + stage * 3 + step - 1,
             )
 
-    def scatter_add(p, stage):
+    def scatter_sum(p, stage):
         axis = ORDERS[p][2 - stage]
+        tiles = 2 if p == 2 else 3
         begin, count = reach(p, stage, at[axis])
         scatter_wait(p, stage)
-
-        def step(four, carry):
-            sums = []
-            for n in range(4):
-                b = four * 4 + n
-                parts = [rstage[stage][p][n * count + b] for n in range(3)]
-                sums.append((b, add_blocks(p, [cs[p][begin + b]] + parts)[1]))
-            for b, block in sums:
-                cs[p][begin + b] = block
-            return carry
-
-        lax.fori_loop(0, count // 4, step, 0)
+        after = accs[p, stage + 1][0 : tiles * 16]
+        tables = [accs[p, stage]] + [ars[p, stage * 3 + n] for n in range(3)]
+        wide_lane = iota((1, count * 128), 1)
+        place_of = begin - core * 64 + wide_lane // 128
+        digits = {
+            ORDERS[p][2]: place_of // 16,
+            ORDERS[p][1]: (place_of // 4) % 4,
+            ORDERS[p][0]: place_of % 4,
+        }
+        packed_lane = (wide_lane % 128) // 64 * 64 + digits["z"] * 16 + digits["y"] * 4 + digits["x"]
+        spread_hot = jnp.where(iota((128, count * 128), 0) == packed_lane, 1.0, 0.0).astype(BF16)
+        factors = [
+            nn(jnp.exp(table[0 : tiles * 16] - after).astype(BF16), spread_hot) for table in tables
+        ]
+        sums = []
+        for b in range(count):
+            blocks = [cs[p][begin + b]] + [rstage[stage][p][n * count + b] for n in range(3)]
+            cols = []
+            for cc in range(tiles):
+                total = jnp.zeros((16, 128), F32)
+                for block, factor in zip(blocks, factors):
+                    part = factor[cc * 16 : cc * 16 + 16, b * 128 : b * 128 + 128]
+                    total = total + block[:, cc * 128 : cc * 128 + 128].astype(F32) * part
+                cols.append(total)
+            sums.append(cols)
+        return begin, sums
+
+    def scatter_add(p, stage):
+        begin, sums = scatter_sum(p, stage)
+        for b, cols in enumerate(sums):
+            cs[p][begin + b] = jnp.concatenate(cols, axis=1).astype(BF16)
+
+    def final_copy(p):
+        return remote(accs.at[p, 3], fin.at[p], FIN + p, sibling)
 
     def scatter_set(n, carry):
         for p in range(3):
@@ -710,6 +682,17 @@
                 def _():
                     swap_finish(2, n - 1)
 
+        for stage in range(3):
+
+            @pl.when(n == stage)
+            def _(stage=stage):
+                table_finish(stage)
+                if stage < 2:
+                    table_start(stage + 1)
+                else:
+                    for p in range(3):
+                        final_copy(p).start()
+
         return carry
 
     lax.fori_loop(0, 4, scatter_set, 0)
@@ -717,6 +700,63 @@
     for p in range(3):
         started.extend(swap_copy(p, n) for n in range(4))
         started.extend(scatter_copy(p, 0, step) for step in (1, 2, 3))
+
+    for p in range(3):
+        started.extend(table_copy(p, stage, step) for stage in range(3) for step in (1, 2, 3))
+        started.append(final_copy(p))
+
+    for p in range(3):
+        arrived(fin.at[p], FIN + p)
+    own_sum = jnp.concatenate([accs[0, 3], accs[1, 3], accs[2, 3]], axis=0)
+    other_sum = jnp.concatenate([fin[0], fin[1], fin[2]], axis=0)
+    zero_sum = jnp.where(core == 0, own_sum, other_sum)
+    one_sum = jnp.where(core == 0, other_sum, own_sum)
+    first_half = jnp.where(low_lanes, zero_sum, pltpu.roll(one_sum, 64, 1))
+    second_half = jnp.where(low_lanes, pltpu.roll(zero_sum, 64, 1), one_sum)
+    log_sum = jnp.concatenate([first_half[0:128], second_half[0:128]], axis=0)
+    raw = jnp.concatenate([first_half[128:144], second_half[128:144]], axis=0)
+    targets = []
+    for g in range(4):
+        chosen = jnp.where(sub == lam_ref[g : g + 1, :], 1.0, 0.0)
+        mass = jnp.exp(s_buf[g] - nn(log_sum, chosen, HIGHEST))
+        mass = jnp.sum(mass, axis=0, keepdims=True)
+        own = iota((16, 128), 1) // 8 == iota((16, 128), 0)
+        targets.append(jnp.sum(jnp.where(own, mass, 0.0), axis=1, keepdims=True))
+    target = jnp.concatenate(targets, axis=0) * (1.0 / 256.0)
+    top = jnp.max(raw, axis=0, keepdims=True)
+    log_prob_all = raw - top - jnp.log(jnp.sum(jnp.exp(raw - top), axis=0, keepdims=True))
+    hot_k = jnp.where(iota((64, 32), 1) == k_col, 1.0, 0.0)
+    log_prob = jnp.sum(
+        jnp.where(one_hot_i, nn(hot_k, log_prob_all, HIGHEST), 0.0), axis=1, keepdims=True
+    )
+    term = jnp.where(valid, target * (jnp.log(target) - log_prob), 0.0)
+    loss_row = jnp.sum(jnp.where(one_hot_i, term, 0.0), axis=0, keepdims=True)
+
+    def loss_start(stage):
+        if stage == 0:
+            start(e_ref.at[0], e_in.at[0], LOSS, sibling)
+            for step in (1, 2, 3):
+                start(e_ref.at[0], e_in.at[step], LOSS + step, peer("x", step))
+                start(e_ref.at[0], e_in.at[3 + step], LOSS + 3 + step, cross(step))
+        else:
+            for step in (1, 2, 3):
+                n = 3 + stage * 3 + step
+                start(e_ref.at[stage], e_in.at[n], LOSS + n, peer("xyz"[stage], step))
+
+    def loss_sum(stage):
+        total = e_ref[stage]
+        for n in range(7) if stage == 0 else range(4 + stage * 3, 7 + stage * 3):
+            arrived(e_in.at[n], LOSS + n)
+            total = total + e_in[n]
+        return total
+
+    e_ref[0] = jnp.broadcast_to(loss_row, (8, 128))
+    loss_start(0)
+    for p in range(3):
+        scatter_add(p, 0)
+        scatter_start(p, 1)
+    e_ref[1] = loss_sum(0)
+    loss_start(1)
 
     coefficient = (LOSS_WEIGHT * E ** (-0.5)) * (jnp.exp(log_prob) - target)
     grads = jnp.where(valid, coefficient * emb, 0.0).astype(BF16)
@@ -724,24 +764,18 @@
     grad_ref[...] = nn(hot_row_t, grads)
 
     for p in range(3):
-        scatter_add(p, 0)
-        scatter_start(p, 1)
-    for p in range(3):
         scatter_add(p, 1)
         scatter_start(p, 2)
-    for p in range(3):
-        begin, _ = reach(p, 2, at[ORDERS[p][0]])
-        scatter_wait(p, 2)
-        total, _ = add_blocks(p, [cs[p][begin]] + [rstage[2][p][n] for n in range(3)])
-        for cc in range(2 if p == 2 else 3):
+    e_ref[2] = loss_sum(1)
+    loss_start(2)
+    for p in range(3):
+        _, sums = scatter_sum(p, 2)
+        for cc, total in enumerate(sums[0]):
             c = 3 * p + cc
-            cols = total[:, cc * 128 : cc * 128 + 128].astype(BF16)
-            ctx_ref[0, :, c * 128 : c * 128 + 128] = total[0:8, cc * 128 : cc * 128 + 128].astype(BF16)
-            ctx_ref[0, :, 1024 + c * 128 : 1152 + c * 128] = total[
-                8:16, cc * 128 : cc * 128 + 128
-            ].astype(BF16)
-        if p == 2:
-            loss_ref[...] = total[0:8, 256:384] + total[8:16, 256:384]
+            ctx_ref[0, :, c * 128 : c * 128 + 128] = total[0:8].astype(BF16)
+            ctx_ref[0, :, 1024 + c * 128 : 1152 + c * 128] = total[8:16].astype(BF16)
+    loss_all = jnp.sum(jnp.where(lane == mine[0], loss_sum(2)[0:1, :], 0.0), axis=1, keepdims=True)
+    loss_ref[...] = jnp.broadcast_to(loss_all, (8, 128))
 
     for copy in started:
         copy.wait_send()
@@ -776,25 +810,24 @@
         pltpu.VMEM((512, 2 * D), BF16),
         pltpu.VMEM((D, 512), BF16),
     ]
-    scratch += [pltpu.VMEM((128, 16, 384), BF16)] * 6
-    scratch += [pltpu.VMEM((64, 16, 384), BF16)] * 3
-    scratch += [pltpu.VMEM((48, 16, 384), BF16)] * 3
-    scratch += [pltpu.VMEM((12, 16, 384), BF16)] * 3
-    scratch += [pltpu.VMEM((3, 16, 384), BF16)] * 3
+    scratch += [pltpu.VMEM((128, 16, 384), BF16)] * 3
+    for blocks in (128, 64, 48, 12, 3):
+        scratch += [pltpu.VMEM((blocks, 16, lanes), BF16) for lanes in (384, 384, 256)]
     scratch += [pltpu.VMEM((4, 256, 128), F32), pltpu.VMEM((4, 256, 128), BF16)]
-    sizes = (64, 64, 16)
-    scratch += [pltpu.VMEM((2 * n, 128), F32) for n in sizes]
-    scratch += [pltpu.VMEM((n, 128), F32) for n in sizes]
-    scratch += [pltpu.VMEM((9, n, 128), F32) for n in sizes]
-    scratch += [pltpu.VMEM((3, n, 128), F32) for n in sizes]
-    scratch += [pltpu.VMEM((2 * n, 128), F32) for n in sizes]
     scratch += [
+        pltpu.VMEM((288, 128), F32),
+        pltpu.VMEM((288, 128), F32),
+        pltpu.VMEM((3, 4, 48, 128), F32),
+        pltpu.VMEM((3, 9, 48, 128), F32),
+        pltpu.VMEM((3, 48, 128), F32),
+        pltpu.VMEM((3, 8, 128), F32),
+        pltpu.VMEM((13, 8, 128), F32),
         pltpu.VMEM((4, 32, 128), jnp.int32),
+        pltpu.VMEM((8, 128), jnp.int32),
         pltpu.VMEM((8, 128), jnp.int32),
         pltpu.VMEM((8, 128), jnp.int32),
         pltpu.VMEM((16, 128), jnp.int32),
         pltpu.SMEM((16, 128), jnp.int32),
-        pltpu.VMEM((128, 128), F32),
         pltpu.SemaphoreType.DMA((SEMS,)),
         pltpu.SemaphoreType.DMA((SEMS,)),
         pltpu.SemaphoreType.DMA((10,)),

time: 85.8 us -> 80.4 us (0.937)
  Pallas kernels: 84.4 us -> 79.5 us
    pallas_call x1, Pallas kernels: 82.7 us -> 77.8 us  [body(): pl.pallas_call(kernel, out_shape=(jax.ShapeDtypeStruct((1, 8, D), BF16),...]
where the time goes in v5:
time: 80.4 us; the launch traced here: 80.3 us
  Pallas kernels  79.5 us (99%)
    pallas_call x1, Pallas kernels, body(): pl.pallas_call(kernel, out_shape=(jax.ShapeDtypeStruct((1, 8, D), BF16),...  77.8 us
    pallas_call x1, Pallas kernels, body(): pl.pallas_call(hand_over, out_shape=(jax.ShapeDtypeStruct((1, 8, D), BF16...  1.65 us

profile of v5, /device:TPU:0, one launch (start us, length us, event | category | flops | bytes accessed | tf_op | source)
XLA Modules:
  0.0 80.3 jit_solution(15528566788189132415)
XLA Ops:
  0.6 77.8 %shard_map.121 = (bf16[1,8,2048]{2,1,0:T(8,128)(2,1)}, f32[8,128]{1,0:T(8,128)}, f32[64,768]{1,0:T(8,128)}) custom-call(s32[32,128]{1,0:T(8,128)} %bitcast.4, s32[64,128]{1,0:T(8,128)} %bitcast.3, s32[1,32]{1,0:T(1,128)} %rq_ref.1, bf16[64,8,2048]{2,1,0:T(8,128)(2,1)} %states_ref.1, bf16[64,768]{1,0:T(8,128)(2,1)} %keys_ref.1, ...), custom_call_target="tpu_custom_call" | custom-call | flops 12000000000 | bytes 20000000 | tf_op jit(solution)/shard_map/pallas_call | solution.py:835
  78.5 1.7 %shard_map.122 = (bf16[1,8,2048]{2,1,0:T(8,128)(2,1)}, f32[1]{0:T(128)}, f32[64,768]{1,0:T(8,128)}) custom-call(bf16[1,8,2048]{2,1,0:T(8,128)(2,1)} %get-tuple-element.6.ctx_ref, f32[8,128]{1,0:T(8,128)} %get-tuple-element.7.loss_ref, f32[64,768]{1,0:T(8,128)} %get-tuple-element.8.grad_ref), custom_call_target="tpu_custom_call" | custom-call | tf_op jit(solution)/shard_map/pallas_call | solution.py:874

commit v6 on v5

--- a/solution.py
+++ b/solution.py
@@ -75,8 +75,8 @@
     grad_ref,
     st,
     w,
-    stored,
-    pick,
+    row_ref,
+    row_smem,
     nrm,
     kv,
     keys_t,
@@ -269,13 +269,9 @@
         code_row = jnp.sum(spread[g * 32 : g * 32 + 32], axis=0, keepdims=True)
         lane_ref[g : g + 1, :] = jnp.where(code_row > 0, code_row // 4096, -1)
         code_cols.append(jnp.sum(jnp.where(slot16, code_row, 0), axis=1, keepdims=True))
-        long_col = jnp.sum(jnp.where(sub == lanes, code_row, 0), axis=1, keepdims=True)
-        token = jnp.where(
-            long_col > 0, (long_col % 128 - 1) * 8 + iota((128, 1), 0) % 8, 512
-        )
-        pick[g * 128 : g * 128 + 128, :] = jnp.where(
-            iota((128, 512), 1) == token, 1.0, 0.0
-        ).astype(BF16)
+        row_ref[g : g + 1, :] = jnp.maximum(code_row % 128 - 1, 0)
+    row_copy = pltpu.make_async_copy(row_ref, row_smem, local_sem.at[10])
+    row_copy.start()
     code_col = jnp.concatenate(code_cols, axis=0)
     valid = code_col > 0
     k_col = (code_col // 128) % 32
@@ -285,6 +281,22 @@
     k_row = (code_row64 // 128) % 32
     row_row = code_row64 % 128 - 1
 
+    states_copy.wait()
+
+    row_copy.wait()
+
+    def norm_slots(four, carry):
+        both = []
+        for n in range(4):
+            values = st[row_smem[four // 4, (four % 4) * 32 + n * 8]].astype(F32)
+            mean_square = jnp.mean(values * values, axis=-1, keepdims=True)
+            both.append(values * lax.rsqrt(mean_square + EPS) * gain_ref[...])
+        rows = pl.ds(pl.multiple_of(four * 32, 32), 32)
+        nrm[rows, :] = jnp.concatenate(both, axis=0).astype(BF16)
+        return carry
+
+    lax.fori_loop(0, 16, norm_slots, 0)
+
     for p in range(3):
         for step in (1, 2, 3):
             gather_wait(p, 1, step)
@@ -305,27 +317,6 @@
     block_copy = pltpu.make_async_copy(block_ref, block_smem, local_sem.at[9])
     block_copy.start()
 
-    states_copy.wait()
-
-    def norm_pair(pair, carry):
-        both = []
-        for half in range(2):
-            values = st[pair * 2 + half].astype(F32)
-            mean_square = jnp.mean(values * values, axis=-1, keepdims=True)
-            both.append(values * lax.rsqrt(mean_square + EPS) * gain_ref[...])
-        rows = pl.ds(pl.multiple_of(pair * 16, 16), 16)
-        stored[rows, :] = jnp.concatenate(both, axis=0).astype(BF16)
-        return carry
-
-    lax.fori_loop(0, 32, norm_pair, 0)
-
-    def pick_step(n, carry):
-        cols = pl.ds(pl.multiple_of(n * 256, 256), 256)
-        nrm[:, cols] = nn(pick[...], stored[:, cols]).astype(BF16)
-        return carry
-
-    lax.fori_loop(0, 8, pick_step, 0)
-
     def project(begin, end):
         def step(n, carry):
             offset = pl.multiple_of(n * 256, 256)
@@ -343,7 +334,7 @@
             forward(p, step)
     def turn(n, carry):
         rows = pl.ds(pl.multiple_of(n * 256, 256), 256)
-        keys_t[rows, :] = jnp.transpose(kv[:, rows].astype(F32)).astype(BF16)
+        keys_t[rows, :] = jnp.transpose(kv[:, rows])
         return carry
 
     lax.fori_loop(0, 8, turn, 0)
@@ -505,7 +496,8 @@
 
     for g in range(4):
         chosen = jnp.where(sub == lam_ref[g : g + 1, :], 1.0, 0.0)
-        p_buf[g] = jnp.exp(s_buf[g] - nn(pair, chosen, HIGHEST)).astype(BF16)
+        used = jnp.broadcast_to(lam_ref[g : g + 1, :] >= 0, (256, 128))
+        p_buf[g] = jnp.where(used, jnp.exp(s_buf[g] - nn(pair, chosen, HIGHEST)), 0.0).astype(BF16)
 
     keep_low = jnp.broadcast_to(lane < 64, (8, 128))
 
@@ -804,8 +796,8 @@
     scratch = [
         pltpu.VMEM((64, 8, D), BF16),
         pltpu.VMEM((D, 2 * D), BF16),
-        pltpu.VMEM((512, D), BF16),
-        pltpu.VMEM((512, 512), BF16),
+        pltpu.VMEM((8, 128), jnp.int32),
+        pltpu.SMEM((8, 128), jnp.int32),
         pltpu.VMEM((512, D), BF16),
         pltpu.VMEM((512, 2 * D), BF16),
         pltpu.VMEM((D, 512), BF16),
@@ -830,7 +822,7 @@
         pltpu.SMEM((16, 128), jnp.int32),
         pltpu.SemaphoreType.DMA((SEMS,)),
         pltpu.SemaphoreType.DMA((SEMS,)),
-        pltpu.SemaphoreType.DMA((10,)),
+        pltpu.SemaphoreType.DMA((11,)),
     ]
     context, loss, grad = pl.pallas_call(
         kernel,

time: 80.4 us -> 79.7 us (level)
  no operation moved by 1% of the time
where the time goes in v6:
time: 79.7 us; the launch traced here: 79.5 us
  Pallas kernels  78.7 us (99%)
  between operations  0.8 us (1%)
    pallas_call x1, Pallas kernels, body(): pl.pallas_call(kernel, out_shape=(jax.ShapeDtypeStruct((1, 8, D), BF16),...  77 us
    pallas_call x1, Pallas kernels, body(): pl.pallas_call(hand_over, out_shape=(jax.ShapeDtypeStruct((1, 8, D), BF16...  1.65 us

profile of v6, /device:TPU:0, one launch (start us, length us, event | category | flops | bytes accessed | tf_op | source)
XLA Modules:
  0.0 79.5 jit_solution(11787128971638803954)
XLA Ops:
  0.6 77.0 %shard_map.121 = (bf16[1,8,2048]{2,1,0:T(8,128)(2,1)}, f32[8,128]{1,0:T(8,128)}, f32[64,768]{1,0:T(8,128)}) custom-call(s32[32,128]{1,0:T(8,128)} %bitcast.4, s32[64,128]{1,0:T(8,128)} %bitcast.3, s32[1,32]{1,0:T(1,128)} %rq_ref.1, bf16[64,8,2048]{2,1,0:T(8,128)(2,1)} %states_ref.1, bf16[64,768]{1,0:T(8,128)(2,1)} %keys_ref.1, ...), custom_call_target="tpu_custom_call" | custom-call | flops 12000000000 | bytes 20000000 | tf_op jit(solution)/shard_map/pallas_call | solution.py:827
  77.7 1.7 %shard_map.122 = (bf16[1,8,2048]{2,1,0:T(8,128)(2,1)}, f32[1]{0:T(128)}, f32[64,768]{1,0:T(8,128)}) custom-call(bf16[1,8,2048]{2,1,0:T(8,128)(2,1)} %get-tuple-element.6.ctx_ref, f32[8,128]{1,0:T(8,128)} %get-tuple-element.7.loss_ref, f32[64,768]{1,0:T(8,128)} %get-tuple-element.8.grad_ref), custom_call_target="tpu_custom_call" | custom-call | tf_op jit(solution)/shard_map/pallas_call | solution.py:866
